TPU v7x, 512 devices: a whole 4x4x16 slice. The times are simulated.
512 devices in a mesh: tm: 256 (over z, y, x), state: 2 (over core).
Axes of the slice: x: 4, y: 4, z: 16, core: 2. Of those that a mesh axis runs over, the one named last changes fastest.
Arguments:
- diagonal: float32 [256, 512, 512], P('tm', None, 'state'), as said below
- lower: float32 [256, 512, 512], P('tm', None, 'state'), as said below
- rhs: float32 [256, 512, 128], P('tm', None, 'state'), may hold values from -6 to 6
Outputs:
- reduced_diagonal: float32 [256, 512, 512], P('tm', None, 'state')
- reduced_lower: float32 [256, 512, 512], P('tm', None, 'state')
- reduced_rhs: float32 [256, 512, 128], P('tm', None, 'state')
Inputs may be any that keep to these rules, and one draw needn't show every extreme that they name: Every diagonal block is symmetric and positive definite, and the whole system is positive definite. `lower`: each coupling block is a full matrix; together with the diagonal blocks it forms the positive definite system.
All inputs are finite; a program needn't handle non-finite values.
Results may differ from a plain program's by a relative error of at most 0.0003.
Values sent between devices are 32-bit elements; how exact they have to be, the bound alone decides.
A program may use at most 64 MiB of HBM per device.

v0:
```python
import functools

import jax
import jax.numpy as jnp
from jax import lax
from jax.experimental import pallas as pl
from jax.experimental.pallas import tpu as pltpu
from jax.sharding import PartitionSpec as P

MESH = pl.DeviceIdType.MESH
F32 = jnp.float32
BF16 = jnp.bfloat16
VMEM = pltpu.VMEM
VMEM_LIMIT = 24 * 1024 * 1024

NN = (((1,), (0,)), ((), ()))
NT = (((1,), (1,)), ((), ()))
TN = (((0,), (0,)), ((), ()))

TOLERANCE = 4e-3
MAX_STEPS = 30


def halves(x):
    high = x.astype(BF16)
    return high, (x - high.astype(F32)).astype(BF16)


def dot1(a, b, dims=NN):
    return lax.dot_general(a, b, dims, preferred_element_type=F32)


def dot3(a, b, dims=NN):
    return dot1(a[0], b[0], dims) + (dot1(a[0], b[1], dims) + dot1(a[1], b[0], dims))


def neighbours(stride):
    length = lax.axis_size("tm")
    row = lax.axis_index("tm")
    core = lax.axis_index("state")
    up = (lax.rem(row + stride, length), core)
    down = (lax.rem(row + length - stride, length), core)
    return row, core, up, down, (row, 1 - core)


def greet(devices):
    barrier = pltpu.get_barrier_semaphore()
    for device in devices:
        pl.semaphore_signal(barrier, inc=1, device_id=device, device_id_type=MESH)
    pl.semaphore_wait(barrier, len(devices))


def send(src, dst, sems, at, device):
    copy = pltpu.make_async_remote_copy(
        src_ref=src,
        dst_ref=dst,
        send_sem=sems.at[0, at],
        recv_sem=sems.at[1, at],
        device_id=device,
        device_id_type=MESH,
    )
    copy.start()
    return copy


def join_kernel(part_ref, full_ref, sems, local_sem):
    _, core, _, _, sibling = neighbours(1)
    width = part_ref.shape[1]
    mine = full_ref.at[:, pl.ds(pl.multiple_of(core * width, width), width)]
    greet((sibling,))
    across = send(part_ref, mine, sems, 0, sibling)
    local = pltpu.make_async_copy(part_ref, mine, local_sem)
    local.start()
    across.wait()
    local.wait()


def join(part):
    size, width = part.shape
    return pl.pallas_call(
        join_kernel,
        out_shape=jax.ShapeDtypeStruct((size, 2 * width), F32),
        in_specs=[pl.BlockSpec(memory_space=pltpu.HBM)],
        out_specs=pl.BlockSpec(memory_space=VMEM),
        scratch_shapes=[pltpu.SemaphoreType.DMA((2, 1)), pltpu.SemaphoreType.DMA],
        compiler_params=pltpu.CompilerParams(
            collective_id=0, has_side_effects=True, vmem_limit_bytes=VMEM_LIMIT
        ),
        name="join_halves",
    )(part)


def invert_kernel(d_ref, p_ref, x_ref, a_high, a_low):
    size = d_ref.shape[0]
    rows = lax.broadcasted_iota(jnp.int32, (size, size), 0)
    cols = lax.broadcasted_iota(jnp.int32, (size, size), 1)
    eye = (rows == cols).astype(F32)
    diag = d_ref[...] * eye
    scale_row = lax.rsqrt(jnp.sum(diag, axis=0, keepdims=True))
    scale_col = lax.rsqrt(jnp.sum(diag, axis=1, keepdims=True))

    def scaled():
        return d_ref[...] * scale_col * scale_row

    a = scaled()
    high, low = halves(a)
    a_high[...] = high
    a_low[...] = low
    off = a - eye
    off_high = off.astype(BF16)
    square = dot1(off_high, off_high)
    top = 1.0 + jnp.sqrt(jnp.sqrt(jnp.sum(square * square))) * 1.01
    bottom = top * (1.0 / 12.0)
    ratio = (top - bottom) / (top + bottom)
    spread = ratio * ratio / (2.0 - ratio * ratio)
    half_sum = 0.5 * (top + bottom)
    gain = 2.0 / (2.0 - ratio * ratio)
    alpha = 2.0 * gain / half_sum
    beta = -gain / (half_sum * half_sum)
    x = (alpha + beta) * eye + beta * off
    resid = (1.0 - alpha - beta) * eye - (alpha + 2.0 * beta) * off - beta * square
    gain = 2.0 / (2.0 - spread * spread)
    x = gain * (x + dot1(x.astype(BF16), resid.astype(BF16)))
    spread = spread * spread / (2.0 - spread * spread)
    gain = 2.0 / (2.0 - spread * spread)
    x_high = x.astype(BF16)
    resid = eye - dot1(a_high[...], x_high)
    x_ref[...] = gain * (x + dot1(x_high, resid.astype(BF16)))

    def going(state):
        step, norm = state
        return jnp.logical_and(step < MAX_STEPS, norm >= TOLERANCE * TOLERANCE)

    def newton(state):
        step, _ = state
        x = x_ref[...]
        x_parts = halves(x)
        resid = eye - dot3((a_high[...], a_low[...]), x_parts)
        x_ref[...] = x + dot1(x_parts[0], resid.astype(BF16))
        return step + 1, jnp.sum(resid * resid)

    _, norm = lax.while_loop(going, newton, (jnp.int32(0), jnp.float32(1.0)))
    converged = norm < TOLERANCE * TOLERANCE

    @pl.when(jnp.logical_not(converged))
    def _():
        x_ref[...] = scaled()

        def eliminate(k, carry):
            block = x_ref[...]
            row = x_ref[pl.ds(k, 1), :]
            lane = lax.broadcasted_iota(jnp.int32, (1, size), 1) == k
            pivot = jnp.sum(jnp.where(lane, row, 0.0), axis=1, keepdims=True)
            row = jnp.where(lane, 1.0, row) / pivot
            column = jnp.sum(jnp.where(lane, block, 0.0), axis=1, keepdims=True)
            x_ref[...] = jnp.where(lane, 0.0, block) - column * row
            x_ref[pl.ds(k, 1), :] = row
            return carry

        lax.fori_loop(0, size, eliminate, 0)

    p_ref[...] = x_ref[...] * scale_col * scale_row


def invert(diag):
    size = diag.shape[0]
    return pl.pallas_call(
        invert_kernel,
        out_shape=jax.ShapeDtypeStruct((size, size), F32),
        in_specs=[pl.BlockSpec(memory_space=VMEM)],
        out_specs=pl.BlockSpec(memory_space=VMEM),
        scratch_shapes=[
            VMEM((size, size), F32),
            VMEM((size, size), BF16),
            VMEM((size, size), BF16),
        ],
        cost_estimate=pl.CostEstimate(
            flops=24 * size**3, bytes_accessed=8 * size * size, transcendentals=0
        ),
        compiler_params=pltpu.CompilerParams(vmem_limit_bytes=VMEM_LIMIT),
        name="invert_block",
    )(diag)


BLOCK = 128
PIECES = 5


def piece(ref, first_row, core, k):
    own, other = 2 * core, 2 - 2 * core
    row = (0, 0, 1, core, 1)[k]
    col = (own, own + 1, own + 1, other, other + core)[k]
    row = pl.multiple_of(first_row + row * BLOCK, BLOCK)
    col = pl.multiple_of(col * BLOCK, BLOCK)
    return ref.at[pl.ds(row, BLOCK), pl.ds(col, BLOCK)]


PLACES = (((0, 0), (0, 1), (1, 1), (0, 2), (1, 2)), ((2, 2), (2, 3), (3, 3), (3, 0), (3, 1)))


def unpack(pieces, full):
    for core in range(2):
        for k in range(PIECES):
            row, col = PLACES[core][k]
            value = pieces[core, k]
            full[row * BLOCK : (row + 1) * BLOCK, col * BLOCK : (col + 1) * BLOCK] = value
            if row != col:
                full[col * BLOCK : (col + 1) * BLOCK, row * BLOCK : (row + 1) * BLOCK] = value.T


def level_kernel(stride, last, *refs):
    ins = 4 if last else 5
    p_ref, low_ref, diag_ref, rhs_ref = refs[:4]
    diag_out, rhs_out, product_out = refs[ins : ins + 3]
    low_full, p_in, p_full, t_own, t_in, t_full, t_rhs_in, rhs_in, sems = refs[ins + 3 :]
    length = lax.axis_size("tm")
    row, core, up, down, sibling = neighbours(stride)
    size, width = low_ref.shape
    first = pl.multiple_of(core * width, width)
    mine = pl.ds(first, width)
    has_up = has_above = row + stride < length
    has_down = has_below = row >= stride

    barrier = pltpu.get_barrier_semaphore()

    def signal(device):
        pl.semaphore_signal(barrier, inc=1, device_id=device, device_id_type=MESH)

    signal(sibling)
    pl.when(has_up)(lambda: signal(up))
    pl.when(has_down)(lambda: signal(down))
    low_full[:, mine] = low_ref[...]
    pl.semaphore_wait(
        barrier, 1 + has_up.astype(jnp.int32) + has_down.astype(jnp.int32)
    )

    def copy(src, dst, at, device):
        return pltpu.make_async_remote_copy(
            src_ref=src,
            dst_ref=dst,
            send_sem=sems.at[0, at],
            recv_sem=sems.at[1, at],
            device_id=device,
            device_id_type=MESH,
        )

    p_up = [copy(piece(p_ref, first, core, k), p_in.at[core, k], k, up) for k in range(PIECES)]
    p_across = [
        copy(p_in.at[core, k], p_in.at[core, k], PIECES + k, sibling) for k in range(PIECES)
    ]
    t_down = [
        copy(piece(t_own, 0, core, k), t_in.at[core, k], 2 * PIECES + k, down)
        for k in range(PIECES)
    ]
    t_across = [
        copy(t_in.at[core, k], t_in.at[core, k], 3 * PIECES + k, sibling) for k in range(PIECES)
    ]
    rhs_up = copy(rhs_ref, rhs_in, 4 * PIECES, up)
    t_rhs_down = copy(t_own.at[width:], t_rhs_in, 4 * PIECES + 1, down)
    low_across = copy(low_ref, low_full.at[:, mine], 4 * PIECES + 2, sibling)

    def each(copies, call):
        for one in copies:
            getattr(one, call)()

    low_across.start()
    pl.when(has_up)(lambda: each(p_up + [rhs_up], "start"))
    own = halves(jnp.concatenate([low_ref[...].T, rhs_ref[...]], axis=0))
    own = halves(dot3(own, halves(p_ref[...])))
    low_across.wait()
    low = halves(low_full[...])
    t_own[...] = dot3(own, low)
    pl.when(has_down)(lambda: each(t_down + [t_rhs_down], "start"))

    @pl.when(has_below)
    def _():
        for k in range(PIECES):
            p_up[k].wait_recv()
            p_across[k].start()
        each(p_across, "wait_recv")

    unpack(p_in, p_full)
    carried = dot3(low, halves(p_full[...]))
    if last:
        product_out[...] = carried
    carried = halves(carried)
    from_diag = dot3(carried, low, NT)
    rest = diag_ref[...] - jnp.where(has_below, from_diag, 0.0)
    if not last:
        from_low = dot3(carried, halves(refs[4][...]))
        product_out[...] = jnp.where(row >= 2 * stride, -from_low, 0.0)
    pl.when(has_below)(rhs_up.wait_recv)
    from_rhs = dot3(halves(rhs_in[...]), carried, NT)

    @pl.when(has_above)
    def _():
        for k in range(PIECES):
            t_down[k].wait_recv()
            t_across[k].start()
        each(t_across, "wait_recv")

    unpack(t_in, t_full)
    if last:
        t_full[...] = rest - jnp.where(has_above, t_full[...], 0.0)
        diag_out[...] = t_full[:, mine]
    else:
        diag_out[...] = rest - jnp.where(has_above, t_full[...], 0.0)
    pl.when(has_above)(t_rhs_down.wait_recv)
    rhs_out[...] = (
        rhs_ref[...]
        - jnp.where(has_below, from_rhs, 0.0)
        - jnp.where(has_above, t_rhs_in[...], 0.0)
    )
    pl.when(has_up)(lambda: each(p_up + [rhs_up], "wait_send"))
    pl.when(has_down)(lambda: each(t_down + [t_rhs_down], "wait_send"))
    pl.when(has_below)(lambda: each(p_across, "wait_send"))
    pl.when(has_above)(lambda: each(t_across, "wait_send"))


def level(stride, p, low_cols, diag, rhs, low_prev=None):
    last = low_prev is None
    size, width = low_cols.shape
    seqs = rhs.shape[0]
    full = jax.ShapeDtypeStruct((size, size), F32)
    half = jax.ShapeDtypeStruct((size, width), F32)
    pieces = VMEM((2, PIECES, BLOCK, BLOCK), F32)
    ins = (p, low_cols, diag, rhs) + (() if last else (low_prev,))
    return pl.pallas_call(
        functools.partial(level_kernel, stride, last),
        out_shape=(
            half if last else full,
            jax.ShapeDtypeStruct((seqs, size), F32),
            full if last else half,
        ),
        in_specs=[pl.BlockSpec(memory_space=VMEM)] * len(ins),
        out_specs=[pl.BlockSpec(memory_space=VMEM)] * 3,
        scratch_shapes=[
            VMEM((size, size), F32),
            pieces,
            VMEM((size, size), F32),
            VMEM((width + seqs, size), F32),
            pieces,
            VMEM((size, size), F32),
            VMEM((seqs, size), F32),
            VMEM((seqs, size), F32),
            pltpu.SemaphoreType.DMA((2, 4 * PIECES + 3)),
        ],
        compiler_params=pltpu.CompilerParams(
            collective_id=stride, has_side_effects=True, vmem_limit_bytes=VMEM_LIMIT
        ),
        name="level_%d" % stride,
    )(*ins)


def finish_kernel(stride, carried_ref, low_prev_ref, diag_ref, rhs_ref, diag_out, low_out, rhs_out):
    product = dot3(halves(carried_ref[...]), halves(low_prev_ref[...]))
    low_out[...] = jnp.where(lax.axis_index("tm") >= 2 * stride, -product, 0.0)
    diag_out[...] = diag_ref[...]
    rhs_out[...] = rhs_ref[...]


def finish(stride, carried, low_prev, diag, rhs):
    half = jax.ShapeDtypeStruct(diag.shape, F32)
    return pl.pallas_call(
        functools.partial(finish_kernel, stride),
        out_shape=(half, half, jax.ShapeDtypeStruct(rhs.shape, F32)),
        in_specs=[pl.BlockSpec(memory_space=VMEM)] * 4,
        out_specs=[pl.BlockSpec(memory_space=VMEM)] * 3,
        compiler_params=pltpu.CompilerParams(vmem_limit_bytes=VMEM_LIMIT),
        name="finish",
    )(carried, low_prev, diag, rhs)


def passed_up(array, stride):
    length = lax.axis_size("tm")
    return lax.ppermute(array, "tm", [(i, i + stride) for i in range(length - stride)])


def per_device(diagonal, lower, rhs):
    low_cols, rhs_rows = lower[0], rhs[0].T
    low_prev = passed_up(low_cols, 1)
    diag = join(diagonal[0])
    diag, rhs_rows, low_cols = level(1, invert(diag), low_cols, diag, rhs_rows, low_prev)
    low_prev = passed_up(low_cols, 2)
    diag, rhs_rows, carried = level(2, invert(diag), low_cols, diag, rhs_rows)
    diag, low_cols, rhs_rows = finish(2, carried, low_prev, diag, rhs_rows)
    return diag[None], low_cols[None], rhs_rows.T[None]


def solution(mesh):
    placed = (P("tm", None, "state"),) * 3
    return jax.shard_map(
        per_device, mesh=mesh, in_specs=placed, out_specs=placed, check_vma=False
    )
```

profile of v0, /device:TPU:132, one launch (start us, length us, event | category | flops | bytes accessed | tf_op | source)
XLA Modules:
  0.0 88.7 jit_solution(38036536579552709)
XLA Ops:
  0.6 3.1 %collective-permute-start = (f32[512,256]{1,0:T(8,128)}, f32[512,256]{1,0:T(8,128)S(1)}, u32[]{:S(2)}, u32[]{:S(2)}) collective-permute-start(f32[512,256]{1,0:T(8,128)} %bitcast.11), channel_id=1, source_target_pairs={{0,2},{2,4},{4,6},{6,8},{8,10},{10,12},{12,14},{14,16},{16,18},{18... | collective-permute-start | bytes 1572872 | tf_op jit(solution)/shard_map/ppermute | solution.py:376
  3.7 0.0 copy-start
  3.8 1.0 %copy-done = f32[1,512,256]{2,1,0:T(8,128)S(1)} copy-done((f32[1,512,256]{2,1,0:T(8,128)S(1)}, f32[1,512,256]{2,1,0:T(8,128)}, u32[]{:S(2)}) %copy-start) | copy-done | bytes 524312
  4.8 2.6 %join_halves.1.d_ref.refs_2_ = f32[512,512]{1,0:T(8,128)S(1)} custom-call(f32[512,256]{1,0:T(8,128)S(1)} %bitcast.10), custom_call_target="tpu_custom_call" | custom-call | tf_op jit(solution)/shard_map/join_halves/pallas_call | solution.py:80
  7.4 0.0 copy-start.1
  7.4 0.0 copy-start.2
  7.5 6.5 %invert_block.2.refs_0_ = f32[512,512]{1,0:T(8,128)S(1)} custom-call(f32[512,512]{1,0:T(8,128)S(1)} %join_halves.1.d_ref.refs_2_), custom_call_target="tpu_custom_call" | custom-call | flops 3221225472 | bytes 2097152 | tf_op jit(solution)/shard_map/invert_block/pallas_call | solution.py:167
  14.0 2.4 %collective-permute-done.refs_4_ = f32[512,256]{1,0:T(8,128)S(1)} collective-permute-done((f32[512,256]{1,0:T(8,128)}, f32[512,256]{1,0:T(8,128)S(1)}, u32[]{:S(2)}, u32[]{:S(2)}) %collective-permute-start) | collective-permute-done | bytes 524320 | tf_op jit(solution)/shard_map/ppermute | solution.py:376
  16.4 0.0 copy-done.1
  16.4 0.0 copy-done.2
  16.4 21.8 %level_1.1 = (f32[512,512]{1,0:T(8,128)S(1)}, f32[64,512]{1,0:T(8,128)S(1)}, f32[512,256]{1,0:T(8,128)S(1)}) custom-call(f32[512,512]{1,0:T(8,128)S(1)} %invert_block.2.refs_0_, f32[512,256]{1,0:T(8,128)S(1)} %bitcast.12, f32[512,512]{1,0:T(8,128)S(1)} %join_halves.1.d_ref.refs_2_, f32[64,512]{1,0:T(8,128)S(1)} %bitcast.13, ...), custom_call_target="tpu_custom_call" | custom-call | tf_op jit(solution)/shard_map/level_1/pallas_call | solution.py:328
  38.2 3.2 %collective-permute-start.1 = (f32[512,256]{1,0:T(8,128)S(1)}, f32[512,256]{1,0:T(8,128)S(1)}, u32[]{:S(2)}, u32[]{:S(2)}) collective-permute-start(f32[512,256]{1,0:T(8,128)S(1)} %get-tuple-element.13.refs_1_), channel_id=1, source_target_pairs={{0,4},{2,6},{4,8},{6,10},{8,12},{10,14},{12,16},{14,18},{16,20},{1... | collective-permute-start | bytes 1572872 | tf_op jit(solution)/shard_map/ppermute | solution.py:376
  41.4 7.8 %invert_block.3.refs_0_ = f32[512,512]{1,0:T(8,128)S(1)} custom-call(f32[512,512]{1,0:T(8,128)S(1)} %get-tuple-element.12.d_ref.refs_2_), custom_call_target="tpu_custom_call" | custom-call | flops 3221225472 | bytes 2097152 | tf_op jit(solution)/shard_map/invert_block/pallas_call | solution.py:167
  49.2 37.9 %level_2.1 = (f32[512,256]{1,0:T(8,128)S(1)}, f32[64,512]{1,0:T(8,128)S(1)}, f32[512,512]{1,0:T(8,128)S(1)}) custom-call(f32[512,512]{1,0:T(8,128)S(1)} %invert_block.3.refs_0_, f32[512,256]{1,0:T(8,128)S(1)} %get-tuple-element.13.refs_1_, f32[512,512]{1,0:T(8,128)S(1)} %get-tuple-element.12.d_ref.refs_2_, f32[64,512]{1,0:T(8,128)S(1)} %get-tuple-element.14.refs_3_), custom_call_target="tpu_custom_call" | custom-call | tf_op jit(solution)/shard_map/level_2/pallas_call | solution.py:328
  87.1 0.0 collective-permute-done.1.low_prev_ref
  87.1 1.5 %finish.1 = (f32[512,256]{1,0:T(8,128)}, f32[512,256]{1,0:T(8,128)}, f32[64,512]{1,0:T(8,128)}) custom-call(f32[512,512]{1,0:T(8,128)S(1)} %get-tuple-element.15.carried_ref, f32[512,256]{1,0:T(8,128)S(1)} %collective-permute-done.1.low_prev_ref, f32[512,256]{1,0:T(8,128)S(1)} %get-tuple-element.16.diag_ref, f32[64,512]{1,0:T(8,128)S(1)} %get-tuple-element.17.rhs_ref), custom_call_target="tpu_custom_call" | custom-call | tf_op jit(solution)/shard_map/finish/pallas_call | solution.py:364
Async XLA Ops:
  0.6 15.8 %collective-permute-start = (f32[512,256]{1,0:T(8,128)}, f32[512,256]{1,0:T(8,128)S(1)}, u32[]{:S(2)}, u32[]{:S(2)}) collective-permute-start(f32[512,256]{1,0:T(8,128)} %bitcast.11), channel_id=1, source_target_pairs={{0,2},{2,4},{4,6},{6,8},{8,10},{10,12},{12,14},{14,16},{16,18},{18... | collective-permute-start | bytes 1572872 | tf_op jit(solution)/shard_map/ppermute | solution.py:376
  3.7 1.0 %copy-start = (f32[1,512,256]{2,1,0:T(8,128)S(1)}, f32[1,512,256]{2,1,0:T(8,128)}, u32[]{:S(2)}) copy-start(f32[1,512,256]{2,1,0:T(8,128)} %param.3) | copy-start | bytes 1572868
  7.4 9.0 %copy-start.1 = (f32[1,512,256]{2,1,0:T(8,128)S(1)}, f32[1,512,256]{2,1,0:T(8,128)}, u32[]{:S(2)}) copy-start(f32[1,512,256]{2,1,0:T(8,128)} %param.4) | copy-start | bytes 1572868
  7.4 9.0 %copy-start.2 = (f32[1,512,64]{1,2,0:T(8,128)S(1)}, f32[1,512,64]{1,2,0:T(8,128)}, u32[]{:S(2)}) copy-start(f32[1,512,64]{1,2,0:T(8,128)} %param.5) | copy-start | bytes 393220
  38.2 48.9 %collective-permute-start.1 = (f32[512,256]{1,0:T(8,128)S(1)}, f32[512,256]{1,0:T(8,128)S(1)}, u32[]{:S(2)}, u32[]{:S(2)}) collective-permute-start(f32[512,256]{1,0:T(8,128)S(1)} %get-tuple-element.13.refs_1_), channel_id=1, source_target_pairs={{0,4},{2,6},{4,8},{6,10},{8,12},{10,14},{12,16},{14,18},{16,20},{1... | collective-permute-start | bytes 1572872 | tf_op jit(solution)/shard_map/ppermute | solution.py:376
where the time goes:
time: 88.9 us; the launch traced here: 88.7 us
  Pallas kernels  78.2 us (88%)
  starting transfers between devices  6.29 us (7%)
  waiting for transfers between devices  2.43 us (3%)
  local copies, waits for them, and re-layouts  1.05 us (1%)
    pallas_call x2, Pallas kernels, level(): pl.pallas_call(functools.partial(level_kernel, stride, last), out_shape=(...  59.7 us
    pallas_call x2, Pallas kernels, invert(): pl.pallas_call(invert_kernel, out_shape=jax.ShapeDtypeStruct((size, size)...  14.3 us
    ppermute x2, starting transfers between devices, passed_up(): lax.ppermute(array, 'tm', [(i, i + stride) for i in range(length - stride)])  6.29 us
    pallas_call x1, Pallas kernels, join(): pl.pallas_call(join_kernel, out_shape=jax.ShapeDtypeStruct((size, 2 * wid...  2.64 us
    ppermute x2, waiting for transfers between devices, passed_up(): lax.ppermute(array, 'tm', [(i, i + stride) for i in range(length - stride)])  2.43 us
  transfers between devices with their start and end apart: 2, of which 1 were waited for; matrix products, arithmetic and copies ran while one was open for 0% of the time, Pallas kernels for 62%

commit v1 on v0

--- a/solution.py
+++ b/solution.py
@@ -17,8 +17,8 @@
 NT = (((1,), (1,)), ((), ()))
 TN = (((0,), (0,)), ((), ()))
 
-TOLERANCE = 4e-3
-MAX_STEPS = 30
+TOLERANCE = 6e-5
+MAX_STEPS = 20
 
 
 def halves(x):
@@ -90,7 +90,7 @@
     )(part)
 
 
-def invert_kernel(d_ref, p_ref, x_ref, a_high, a_low):
+def invert_kernel(d_ref, p_ref, inverse_ref, x_ref, a_high, a_low):
     size = d_ref.shape[0]
     rows = lax.broadcasted_iota(jnp.int32, (size, size), 0)
     cols = lax.broadcasted_iota(jnp.int32, (size, size), 1)
@@ -125,41 +125,48 @@
     gain = 2.0 / (2.0 - spread * spread)
     x_high = x.astype(BF16)
     resid = eye - dot1(a_high[...], x_high)
-    x_ref[...] = gain * (x + dot1(x_high, resid.astype(BF16)))
-
-    def going(state):
-        step, norm = state
-        return jnp.logical_and(step < MAX_STEPS, norm >= TOLERANCE * TOLERANCE)
-
-    def newton(state):
+    x_ref[...] = (gain * (x + dot1(x_high, resid.astype(BF16)))).astype(BF16)
+
+    def refine(state):
         step, _ = state
         x = x_ref[...]
-        x_parts = halves(x)
-        resid = eye - dot3((a_high[...], a_low[...]), x_parts)
-        x_ref[...] = x + dot1(x_parts[0], resid.astype(BF16))
-        return step + 1, jnp.sum(resid * resid)
-
-    _, norm = lax.while_loop(going, newton, (jnp.int32(0), jnp.float32(1.0)))
-    converged = norm < TOLERANCE * TOLERANCE
+        resid = eye - (dot1(a_high[...], x) + dot1(a_low[...], x))
+        resid_high = resid.astype(BF16)
+        second = dot1(resid_high, resid_high)
+        bound = jnp.sum(resid * resid) * jnp.sum(second * second)
+        change = halves(resid + second)
+        new = x.astype(F32) + (dot1(x, change[0]) + dot1(x, change[1]))
+        x_ref[...] = new.astype(BF16)
+        inverse_ref[...] = new
+        return step + 1, bound
+
+    limit = TOLERANCE * TOLERANCE * size
+
+    def going(state):
+        step, bound = state
+        return jnp.logical_and(step < MAX_STEPS, bound >= limit)
+
+    _, bound = lax.while_loop(going, refine, refine((jnp.int32(0), jnp.float32(0.0))))
+    converged = bound < limit
 
     @pl.when(jnp.logical_not(converged))
     def _():
-        x_ref[...] = scaled()
+        inverse_ref[...] = scaled()
 
         def eliminate(k, carry):
-            block = x_ref[...]
-            row = x_ref[pl.ds(k, 1), :]
+            block = inverse_ref[...]
+            row = inverse_ref[pl.ds(k, 1), :]
             lane = lax.broadcasted_iota(jnp.int32, (1, size), 1) == k
             pivot = jnp.sum(jnp.where(lane, row, 0.0), axis=1, keepdims=True)
             row = jnp.where(lane, 1.0, row) / pivot
             column = jnp.sum(jnp.where(lane, block, 0.0), axis=1, keepdims=True)
-            x_ref[...] = jnp.where(lane, 0.0, block) - column * row
-            x_ref[pl.ds(k, 1), :] = row
+            inverse_ref[...] = jnp.where(lane, 0.0, block) - column * row
+            inverse_ref[pl.ds(k, 1), :] = row
             return carry
 
         lax.fori_loop(0, size, eliminate, 0)
 
-    p_ref[...] = x_ref[...] * scale_col * scale_row
+    p_ref[...] = inverse_ref[...] * scale_col * scale_row
 
 
 def invert(diag):
@@ -173,6 +180,7 @@
             VMEM((size, size), F32),
             VMEM((size, size), BF16),
             VMEM((size, size), BF16),
+            VMEM((size, size), BF16),
         ],
         cost_estimate=pl.CostEstimate(
             flops=24 * size**3, bytes_accessed=8 * size * size, transcendentals=0
@@ -208,18 +216,24 @@
                 full[col * BLOCK : (col + 1) * BLOCK, row * BLOCK : (row + 1) * BLOCK] = value.T
 
 
-def level_kernel(stride, last, *refs):
-    ins = 4 if last else 5
-    p_ref, low_ref, diag_ref, rhs_ref = refs[:4]
-    diag_out, rhs_out, product_out = refs[ins : ins + 3]
-    low_full, p_in, p_full, t_own, t_in, t_full, t_rhs_in, rhs_in, sems = refs[ins + 3 :]
+def level_kernel(
+    stride, last, p_ref, low_ref, diag_ref, rhs_ref, diag_out, rhs_out, carried_out,
+    low_full, p_in, p_full, t_own, t_in, t_full, t_rhs_in, rhs_in, *rest,
+):
+    relay = stride > 1
+    if relay:
+        p_relay, t_relay, rhs_relay, t_rhs_relay, sems = rest
+    else:
+        (sems,) = rest
     length = lax.axis_size("tm")
-    row, core, up, down, sibling = neighbours(stride)
+    row, core, up, down, sibling = neighbours(1)
     size, width = low_ref.shape
     first = pl.multiple_of(core * width, width)
     mine = pl.ds(first, width)
     has_up = has_above = row + stride < length
     has_down = has_below = row >= stride
+    near_up, near_down = row + 1 < length, row >= 1
+    between = jnp.logical_and(near_up, near_down)
 
     barrier = pltpu.get_barrier_semaphore()
 
@@ -227,14 +241,17 @@
         pl.semaphore_signal(barrier, inc=1, device_id=device, device_id_type=MESH)
 
     signal(sibling)
-    pl.when(has_up)(lambda: signal(up))
-    pl.when(has_down)(lambda: signal(down))
+    pl.when(near_up)(lambda: signal(up))
+    pl.when(near_down)(lambda: signal(down))
     low_full[:, mine] = low_ref[...]
     pl.semaphore_wait(
-        barrier, 1 + has_up.astype(jnp.int32) + has_down.astype(jnp.int32)
+        barrier, 1 + near_up.astype(jnp.int32) + near_down.astype(jnp.int32)
     )
 
-    def copy(src, dst, at, device):
+    used = iter(range(sems.shape[1]))
+
+    def copy(src, dst, device):
+        at = next(used)
         return pltpu.make_async_remote_copy(
             src_ref=src,
             dst_ref=dst,
@@ -244,95 +261,105 @@
             device_id_type=MESH,
         )
 
-    p_up = [copy(piece(p_ref, first, core, k), p_in.at[core, k], k, up) for k in range(PIECES)]
-    p_across = [
-        copy(p_in.at[core, k], p_in.at[core, k], PIECES + k, sibling) for k in range(PIECES)
-    ]
-    t_down = [
-        copy(piece(t_own, 0, core, k), t_in.at[core, k], 2 * PIECES + k, down)
+    def path(src, held, dst, device):
+        if not relay:
+            return [copy(src, dst, device)]
+        return [copy(src, held, device), copy(held, dst, device)]
+
+    p_paths = [
+        path(piece(p_ref, first, core, k), relay and p_relay.at[k], p_in.at[core, k], up)
         for k in range(PIECES)
     ]
-    t_across = [
-        copy(t_in.at[core, k], t_in.at[core, k], 3 * PIECES + k, sibling) for k in range(PIECES)
+    t_paths = [
+        path(piece(t_own, 0, core, k), relay and t_relay.at[k], t_in.at[core, k], down)
+        for k in range(PIECES)
     ]
-    rhs_up = copy(rhs_ref, rhs_in, 4 * PIECES, up)
-    t_rhs_down = copy(t_own.at[width:], t_rhs_in, 4 * PIECES + 1, down)
-    low_across = copy(low_ref, low_full.at[:, mine], 4 * PIECES + 2, sibling)
+    p_paths.append(path(rhs_ref, relay and rhs_relay, rhs_in, up))
+    t_paths.append(path(t_own.at[width:], relay and t_rhs_relay, t_rhs_in, down))
+    p_across = [copy(p_in.at[core, k], p_in.at[core, k], sibling) for k in range(PIECES)]
+    t_across = [copy(t_in.at[core, k], t_in.at[core, k], sibling) for k in range(PIECES)]
+    low_across = copy(low_ref, low_full.at[:, mine], sibling)
 
     def each(copies, call):
         for one in copies:
             getattr(one, call)()
 
     low_across.start()
-    pl.when(has_up)(lambda: each(p_up + [rhs_up], "start"))
+    pl.when(has_up)(lambda: each([way[0] for way in p_paths], "start"))
     own = halves(jnp.concatenate([low_ref[...].T, rhs_ref[...]], axis=0))
     own = halves(dot3(own, halves(p_ref[...])))
     low_across.wait()
     low = halves(low_full[...])
     t_own[...] = dot3(own, low)
-    pl.when(has_down)(lambda: each(t_down + [t_rhs_down], "start"))
+    pl.when(has_down)(lambda: each([way[0] for way in t_paths], "start"))
+
+    if relay:
+
+        @pl.when(between)
+        def _():
+            order = p_paths[:3]
+            for k in range(3):
+                order += [t_paths[k], p_paths[3 + k]]
+            for way in order + t_paths[3:]:
+                way[0].wait_recv()
+                way[1].start()
 
     @pl.when(has_below)
     def _():
         for k in range(PIECES):
-            p_up[k].wait_recv()
+            p_paths[k][-1].wait_recv()
             p_across[k].start()
         each(p_across, "wait_recv")
 
     unpack(p_in, p_full)
     carried = dot3(low, halves(p_full[...]))
-    if last:
-        product_out[...] = carried
+    carried_out[...] = carried
     carried = halves(carried)
     from_diag = dot3(carried, low, NT)
-    rest = diag_ref[...] - jnp.where(has_below, from_diag, 0.0)
-    if not last:
-        from_low = dot3(carried, halves(refs[4][...]))
-        product_out[...] = jnp.where(row >= 2 * stride, -from_low, 0.0)
-    pl.when(has_below)(rhs_up.wait_recv)
+    left = diag_ref[...] - jnp.where(has_below, from_diag, 0.0)
+    pl.when(has_below)(p_paths[PIECES][-1].wait_recv)
     from_rhs = dot3(halves(rhs_in[...]), carried, NT)
 
     @pl.when(has_above)
     def _():
         for k in range(PIECES):
-            t_down[k].wait_recv()
+            t_paths[k][-1].wait_recv()
             t_across[k].start()
         each(t_across, "wait_recv")
 
     unpack(t_in, t_full)
     if last:
-        t_full[...] = rest - jnp.where(has_above, t_full[...], 0.0)
+        t_full[...] = left - jnp.where(has_above, t_full[...], 0.0)
         diag_out[...] = t_full[:, mine]
     else:
-        diag_out[...] = rest - jnp.where(has_above, t_full[...], 0.0)
-    pl.when(has_above)(t_rhs_down.wait_recv)
+        diag_out[...] = left - jnp.where(has_above, t_full[...], 0.0)
+    pl.when(has_above)(t_paths[PIECES][-1].wait_recv)
     rhs_out[...] = (
         rhs_ref[...]
         - jnp.where(has_below, from_rhs, 0.0)
         - jnp.where(has_above, t_rhs_in[...], 0.0)
     )
-    pl.when(has_up)(lambda: each(p_up + [rhs_up], "wait_send"))
-    pl.when(has_down)(lambda: each(t_down + [t_rhs_down], "wait_send"))
+    pl.when(has_up)(lambda: each([way[0] for way in p_paths], "wait_send"))
+    pl.when(has_down)(lambda: each([way[0] for way in t_paths], "wait_send"))
+    if relay:
+        pl.when(between)(lambda: each([way[1] for way in p_paths + t_paths], "wait_send"))
     pl.when(has_below)(lambda: each(p_across, "wait_send"))
     pl.when(has_above)(lambda: each(t_across, "wait_send"))
 
 
-def level(stride, p, low_cols, diag, rhs, low_prev=None):
-    last = low_prev is None
+def level(stride, last, p, low_cols, diag, rhs):
     size, width = low_cols.shape
     seqs = rhs.shape[0]
     full = jax.ShapeDtypeStruct((size, size), F32)
     half = jax.ShapeDtypeStruct((size, width), F32)
     pieces = VMEM((2, PIECES, BLOCK, BLOCK), F32)
-    ins = (p, low_cols, diag, rhs) + (() if last else (low_prev,))
+    vectors = VMEM((seqs, size), F32)
+    relays = [VMEM((PIECES, BLOCK, BLOCK), F32)] * 2 + [vectors] * 2
+    copies = 4 * PIECES + 3 + (2 * PIECES + 2) * (stride > 1)
     return pl.pallas_call(
         functools.partial(level_kernel, stride, last),
-        out_shape=(
-            half if last else full,
-            jax.ShapeDtypeStruct((seqs, size), F32),
-            full if last else half,
-        ),
-        in_specs=[pl.BlockSpec(memory_space=VMEM)] * len(ins),
+        out_shape=(half if last else full, jax.ShapeDtypeStruct((seqs, size), F32), full),
+        in_specs=[pl.BlockSpec(memory_space=VMEM)] * 4,
         out_specs=[pl.BlockSpec(memory_space=VMEM)] * 3,
         scratch_shapes=[
             VMEM((size, size), F32),
@@ -341,20 +368,36 @@
             VMEM((width + seqs, size), F32),
             pieces,
             VMEM((size, size), F32),
-            VMEM((seqs, size), F32),
-            VMEM((seqs, size), F32),
-            pltpu.SemaphoreType.DMA((2, 4 * PIECES + 3)),
+            vectors,
+            vectors,
+            *(relays if stride > 1 else ()),
+            pltpu.SemaphoreType.DMA((2, copies)),
         ],
         compiler_params=pltpu.CompilerParams(
             collective_id=stride, has_side_effects=True, vmem_limit_bytes=VMEM_LIMIT
         ),
         name="level_%d" % stride,
-    )(*ins)
-
-
-def finish_kernel(stride, carried_ref, low_prev_ref, diag_ref, rhs_ref, diag_out, low_out, rhs_out):
+    )(p, low_cols, diag, rhs)
+
+
+def couple_kernel(stride, carried_ref, low_prev_ref, low_out):
     product = dot3(halves(carried_ref[...]), halves(low_prev_ref[...]))
     low_out[...] = jnp.where(lax.axis_index("tm") >= 2 * stride, -product, 0.0)
+
+
+def couple(stride, carried, low_prev):
+    return pl.pallas_call(
+        functools.partial(couple_kernel, stride),
+        out_shape=jax.ShapeDtypeStruct(low_prev.shape, F32),
+        in_specs=[pl.BlockSpec(memory_space=VMEM)] * 2,
+        out_specs=pl.BlockSpec(memory_space=VMEM),
+        compiler_params=pltpu.CompilerParams(vmem_limit_bytes=VMEM_LIMIT),
+        name="couple",
+    )(carried, low_prev)
+
+
+def finish_kernel(stride, carried_ref, low_prev_ref, diag_ref, rhs_ref, diag_out, low_out, rhs_out):
+    couple_kernel(stride, carried_ref, low_prev_ref, low_out)
     diag_out[...] = diag_ref[...]
     rhs_out[...] = rhs_ref[...]
 
@@ -380,9 +423,10 @@
     low_cols, rhs_rows = lower[0], rhs[0].T
     low_prev = passed_up(low_cols, 1)
     diag = join(diagonal[0])
-    diag, rhs_rows, low_cols = level(1, invert(diag), low_cols, diag, rhs_rows, low_prev)
+    diag, rhs_rows, carried = level(1, False, invert(diag), low_cols, diag, rhs_rows)
+    low_cols = couple(1, carried, low_prev)
     low_prev = passed_up(low_cols, 2)
-    diag, rhs_rows, carried = level(2, invert(diag), low_cols, diag, rhs_rows)
+    diag, rhs_rows, carried = level(2, True, invert(diag), low_cols, diag, rhs_rows)
     diag, low_cols, rhs_rows = finish(2, carried, low_prev, diag, rhs_rows)
     return diag[None], low_cols[None], rhs_rows.T[None]
 

time: 88.9 us -> 83.5 us (0.939)
  the two profiles are of different devices: /device:TPU:132 before, /device:TPU:256 now
where the time goes in v1:
time: 83.5 us; the launch traced here: 83.3 us
  Pallas kernels  76.1 us (91%)
  starting transfers between devices  5.32 us (6%)
  local copies, waits for them, and re-layouts  1.05 us (1%)
    pallas_call x2, Pallas kernels, level(): pl.pallas_call(functools.partial(level_kernel, stride, last), out_shape=(...  59.4 us
    pallas_call x2, Pallas kernels, invert(): pl.pallas_call(invert_kernel, out_shape=jax.ShapeDtypeStruct((size, size)...  11.9 us
    ppermute x2, starting transfers between devices, passed_up(): lax.ppermute(array, 'tm', [(i, i + stride) for i in range(length - stride)])  5.32 us
    pallas_call x1, Pallas kernels, join(): pl.pallas_call(join_kernel, out_shape=jax.ShapeDtypeStruct((size, 2 * wid...  2.64 us
  transfers between devices with their start and end apart: 2, of which 0 were waited for; matrix products, arithmetic and copies ran while one was open for 0% of the time, Pallas kernels for 89%

profile of v1, /device:TPU:256, one launch (start us, length us, event | category | flops | bytes accessed | tf_op | source)
XLA Modules:
  0.0 83.3 jit_solution(17737230145011663066)
XLA Ops:
  0.6 3.4 %collective-permute-start = (f32[512,256]{1,0:T(8,128)}, f32[512,256]{1,0:T(8,128)S(1)}, u32[]{:S(2)}, u32[]{:S(2)}) collective-permute-start(f32[512,256]{1,0:T(8,128)} %bitcast.11), channel_id=1, source_target_pairs={{0,2},{2,4},{4,6},{6,8},{8,10},{10,12},{12,14},{14,16},{16,18},{18... | collective-permute-start | bytes 1572872 | tf_op jit(solution)/shard_map/ppermute | solution.py:419
  4.0 0.0 copy-start
  4.0 1.0 %copy-done = f32[1,512,256]{2,1,0:T(8,128)S(1)} copy-done((f32[1,512,256]{2,1,0:T(8,128)S(1)}, f32[1,512,256]{2,1,0:T(8,128)}, u32[]{:S(2)}) %copy-start) | copy-done | bytes 524312
  5.1 2.6 %join_halves.1.d_ref.diag_ref = f32[512,512]{1,0:T(8,128)S(1)} custom-call(f32[512,256]{1,0:T(8,128)S(1)} %bitcast.10), custom_call_target="tpu_custom_call" | custom-call | tf_op jit(solution)/shard_map/join_halves/pallas_call | solution.py:80
  7.7 0.0 copy-start.1
  7.7 0.0 copy-start.2
  7.8 5.9 %invert_block.2.p_ref = f32[512,512]{1,0:T(8,128)S(1)} custom-call(f32[512,512]{1,0:T(8,128)S(1)} %join_halves.1.d_ref.diag_ref), custom_call_target="tpu_custom_call" | custom-call | flops 3221225472 | bytes 2097152 | tf_op jit(solution)/shard_map/invert_block/pallas_call | solution.py:174
  13.6 0.0 copy-done.1
  13.6 0.0 copy-done.2
  13.6 22.2 %level_1.1 = (f32[512,512]{1,0:T(8,128)S(1)}, f32[64,512]{1,0:T(8,128)S(1)}, f32[512,512]{1,0:T(8,128)S(1)}) custom-call(f32[512,512]{1,0:T(8,128)S(1)} %invert_block.2.p_ref, f32[512,256]{1,0:T(8,128)S(1)} %bitcast.12, f32[512,512]{1,0:T(8,128)S(1)} %join_halves.1.d_ref.diag_ref, f32[64,512]{1,0:T(8,128)S(1)} %bitcast.13), custom_call_target="tpu_custom_call" | custom-call | tf_op jit(solution)/shard_map/level_1/pallas_call | solution.py:359
  35.9 0.0 collective-permute-done.low_prev_ref
  35.9 0.6 couple.1.low_ref
  36.5 1.9 %collective-permute-start.1 = (f32[512,256]{1,0:T(8,128)S(1)}, f32[512,256]{1,0:T(8,128)S(1)}, u32[]{:S(2)}, u32[]{:S(2)}) collective-permute-start(f32[512,256]{1,0:T(8,128)S(1)} %couple.1.low_ref), channel_id=1, source_target_pairs={{0,4},{2,6},{4,8},{6,10},{8,12},{10,14},{12,16},{14,18},{16,20},{1... | collective-permute-start | bytes 1572872 | tf_op jit(solution)/shard_map/ppermute | solution.py:419
  38.4 6.1 %invert_block.3.p_ref = f32[512,512]{1,0:T(8,128)S(1)} custom-call(f32[512,512]{1,0:T(8,128)S(1)} %get-tuple-element.12.d_ref.diag_ref), custom_call_target="tpu_custom_call" | custom-call | flops 3221225472 | bytes 2097152 | tf_op jit(solution)/shard_map/invert_block/pallas_call | solution.py:174
  44.4 37.2 %level_2.1 = (f32[512,256]{1,0:T(8,128)S(1)}, f32[64,512]{1,0:T(8,128)S(1)}, f32[512,512]{1,0:T(8,128)S(1)}) custom-call(f32[512,512]{1,0:T(8,128)S(1)} %invert_block.3.p_ref, f32[512,256]{1,0:T(8,128)S(1)} %couple.1.low_ref, f32[512,512]{1,0:T(8,128)S(1)} %get-tuple-element.12.d_ref.diag_ref, f32[64,512]{1,0:T(8,128)S(1)} %get-tuple-element.14.rhs_ref), custom_call_target="tpu_custom_call" | custom-call | tf_op jit(solution)/shard_map/level_2/pallas_call | solution.py:359
  81.7 0.0 collective-permute-done.1.low_prev_ref
  81.7 1.6 %finish.1 = (f32[512,256]{1,0:T(8,128)}, f32[512,256]{1,0:T(8,128)}, f32[64,512]{1,0:T(8,128)}) custom-call(f32[512,512]{1,0:T(8,128)S(1)} %get-tuple-element.15.carried_ref, f32[512,256]{1,0:T(8,128)S(1)} %collective-permute-done.1.low_prev_ref, f32[512,256]{1,0:T(8,128)S(1)} %get-tuple-element.16.diag_ref, f32[64,512]{1,0:T(8,128)S(1)} %get-tuple-element.17.rhs_ref), custom_call_target="tpu_custom_call" | custom-call | tf_op jit(solution)/shard_map/finish/pallas_call | solution.py:407
Async XLA Ops:
  0.6 35.2 %collective-permute-start = (f32[512,256]{1,0:T(8,128)}, f32[512,256]{1,0:T(8,128)S(1)}, u32[]{:S(2)}, u32[]{:S(2)}) collective-permute-start(f32[512,256]{1,0:T(8,128)} %bitcast.11), channel_id=1, source_target_pairs={{0,2},{2,4},{4,6},{6,8},{8,10},{10,12},{12,14},{14,16},{16,18},{18... | collective-permute-start | bytes 1572872 | tf_op jit(solution)/shard_map/ppermute | solution.py:419
  4.0 1.0 %copy-start = (f32[1,512,256]{2,1,0:T(8,128)S(1)}, f32[1,512,256]{2,1,0:T(8,128)}, u32[]{:S(2)}) copy-start(f32[1,512,256]{2,1,0:T(8,128)} %param.3) | copy-start | bytes 1572868
  7.7 5.9 %copy-start.1 = (f32[1,512,256]{2,1,0:T(8,128)S(1)}, f32[1,512,256]{2,1,0:T(8,128)}, u32[]{:S(2)}) copy-start(f32[1,512,256]{2,1,0:T(8,128)} %param.4) | copy-start | bytes 1572868
  7.7 5.9 %copy-start.2 = (f32[1,512,64]{1,2,0:T(8,128)S(1)}, f32[1,512,64]{1,2,0:T(8,128)}, u32[]{:S(2)}) copy-start(f32[1,512,64]{1,2,0:T(8,128)} %param.5) | copy-start | bytes 393220
  36.5 45.2 %collective-permute-start.1 = (f32[512,256]{1,0:T(8,128)S(1)}, f32[512,256]{1,0:T(8,128)S(1)}, u32[]{:S(2)}, u32[]{:S(2)}) collective-permute-start(f32[512,256]{1,0:T(8,128)S(1)} %couple.1.low_ref), channel_id=1, source_target_pairs={{0,4},{2,6},{4,8},{6,10},{8,12},{10,14},{12,16},{14,18},{16,20},{1... | collective-permute-start | bytes 1572872 | tf_op jit(solution)/shard_map/ppermute | solution.py:419

commit v2 on v1

--- a/solution.py
+++ b/solution.py
@@ -191,34 +191,51 @@
 
 
 BLOCK = 128
-PIECES = 5
-
-
-def piece(ref, first_row, core, k):
+PACKED = 4 * BLOCK + 8
+CHUNKS = ((0, 2 * BLOCK), (2 * BLOCK, 2 * BLOCK + 8))
+
+
+def pack(ref, first_row, core, packed):
     own, other = 2 * core, 2 - 2 * core
-    row = (0, 0, 1, core, 1)[k]
-    col = (own, own + 1, own + 1, other, other + core)[k]
-    row = pl.multiple_of(first_row + row * BLOCK, BLOCK)
-    col = pl.multiple_of(col * BLOCK, BLOCK)
-    return ref.at[pl.ds(row, BLOCK), pl.ds(col, BLOCK)]
-
-
-PLACES = (((0, 0), (0, 1), (1, 1), (0, 2), (1, 2)), ((2, 2), (2, 3), (3, 3), (3, 0), (3, 1)))
-
-
-def unpack(pieces, full):
-    for core in range(2):
-        for k in range(PIECES):
-            row, col = PLACES[core][k]
-            value = pieces[core, k]
-            full[row * BLOCK : (row + 1) * BLOCK, col * BLOCK : (col + 1) * BLOCK] = value
-            if row != col:
-                full[col * BLOCK : (col + 1) * BLOCK, row * BLOCK : (row + 1) * BLOCK] = value.T
+
+    def block(row, col):
+        row = pl.multiple_of(first_row + row * BLOCK, BLOCK)
+        col = pl.multiple_of(col * BLOCK, BLOCK)
+        return ref[pl.ds(row, BLOCK), pl.ds(col, BLOCK)]
+
+    packed[:BLOCK] = block(0, own + 1)
+    packed[BLOCK : 2 * BLOCK] = block(core, other)
+    packed[2 * BLOCK : 3 * BLOCK] = block(1, other + core)
+    rows = lax.broadcasted_iota(jnp.int32, (BLOCK, BLOCK), 0)
+    cols = lax.broadcasted_iota(jnp.int32, (BLOCK, BLOCK), 1)
+    second = block(1, own + 1)
+    packed[3 * BLOCK : 4 * BLOCK] = jnp.where(rows >= cols, block(0, own), second)
+    diagonal = jnp.sum(jnp.where(rows == cols, second, 0.0), axis=0, keepdims=True)
+    packed[4 * BLOCK :] = jnp.broadcast_to(diagonal, (8, BLOCK))
+
+
+def unpack(shares, full):
+    def put(row, col, value):
+        full[row * BLOCK : (row + 1) * BLOCK, col * BLOCK : (col + 1) * BLOCK] = value
+
+    rows = lax.broadcasted_iota(jnp.int32, (BLOCK, BLOCK), 0)
+    cols = lax.broadcasted_iota(jnp.int32, (BLOCK, BLOCK), 1)
+    for core, places in enumerate((((0, 1), (0, 2), (1, 2)), ((2, 3), (3, 0), (3, 1)))):
+        for k, (row, col) in enumerate(places):
+            value = shares[core, k * BLOCK : (k + 1) * BLOCK]
+            put(row, col, value)
+            put(col, row, value.T)
+        both = shares[core, 3 * BLOCK : 4 * BLOCK]
+        turned = both.T
+        diagonal = shares[core, 4 * BLOCK : 4 * BLOCK + 1]
+        put(2 * core, 2 * core, jnp.where(rows >= cols, both, turned))
+        second = jnp.where(rows < cols, both, jnp.where(rows > cols, turned, diagonal))
+        put(2 * core + 1, 2 * core + 1, second)
 
 
 def level_kernel(
     stride, last, p_ref, low_ref, diag_ref, rhs_ref, diag_out, rhs_out, carried_out,
-    low_full, p_in, p_full, t_own, t_in, t_full, t_rhs_in, rhs_in, *rest,
+    low_full, p_out, p_in, p_full, t_own, t_out, t_in, t_full, t_rhs_in, rhs_in, *rest,
 ):
     relay = stride > 1
     if relay:
@@ -244,6 +261,7 @@
     pl.when(near_up)(lambda: signal(up))
     pl.when(near_down)(lambda: signal(down))
     low_full[:, mine] = low_ref[...]
+    pack(p_ref, first, core, p_out)
     pl.semaphore_wait(
         barrier, 1 + near_up.astype(jnp.int32) + near_down.astype(jnp.int32)
     )
@@ -266,18 +284,21 @@
             return [copy(src, dst, device)]
         return [copy(src, held, device), copy(held, dst, device)]
 
-    p_paths = [
-        path(piece(p_ref, first, core, k), relay and p_relay.at[k], p_in.at[core, k], up)
-        for k in range(PIECES)
-    ]
-    t_paths = [
-        path(piece(t_own, 0, core, k), relay and t_relay.at[k], t_in.at[core, k], down)
-        for k in range(PIECES)
-    ]
+    def packed_paths(out, held, into, device):
+        return [
+            path(out.at[pl.ds(at, n)], relay and held.at[pl.ds(at, n)], into.at[core, pl.ds(at, n)], device)
+            for at, n in CHUNKS
+        ]
+
+    def packed_across(into):
+        parts = [into.at[core, pl.ds(at, n)] for at, n in CHUNKS]
+        return [copy(part, part, sibling) for part in parts]
+
+    p_paths = packed_paths(p_out, relay and p_relay, p_in, up)
+    t_paths = packed_paths(t_out, relay and t_relay, t_in, down)
     p_paths.append(path(rhs_ref, relay and rhs_relay, rhs_in, up))
     t_paths.append(path(t_own.at[width:], relay and t_rhs_relay, t_rhs_in, down))
-    p_across = [copy(p_in.at[core, k], p_in.at[core, k], sibling) for k in range(PIECES)]
-    t_across = [copy(t_in.at[core, k], t_in.at[core, k], sibling) for k in range(PIECES)]
+    p_across, t_across = packed_across(p_in), packed_across(t_in)
     low_across = copy(low_ref, low_full.at[:, mine], sibling)
 
     def each(copies, call):
@@ -291,24 +312,22 @@
     low_across.wait()
     low = halves(low_full[...])
     t_own[...] = dot3(own, low)
+    pack(t_own, 0, core, t_out)
     pl.when(has_down)(lambda: each([way[0] for way in t_paths], "start"))
 
     if relay:
 
         @pl.when(between)
         def _():
-            order = p_paths[:3]
-            for k in range(3):
-                order += [t_paths[k], p_paths[3 + k]]
-            for way in order + t_paths[3:]:
+            for way in p_paths[:2] + t_paths[:1] + p_paths[2:] + t_paths[1:]:
                 way[0].wait_recv()
                 way[1].start()
 
     @pl.when(has_below)
     def _():
-        for k in range(PIECES):
-            p_paths[k][-1].wait_recv()
-            p_across[k].start()
+        for way, across in zip(p_paths, p_across):
+            way[-1].wait_recv()
+            across.start()
         each(p_across, "wait_recv")
 
     unpack(p_in, p_full)
@@ -317,14 +336,14 @@
     carried = halves(carried)
     from_diag = dot3(carried, low, NT)
     left = diag_ref[...] - jnp.where(has_below, from_diag, 0.0)
-    pl.when(has_below)(p_paths[PIECES][-1].wait_recv)
+    pl.when(has_below)(p_paths[-1][-1].wait_recv)
     from_rhs = dot3(halves(rhs_in[...]), carried, NT)
 
     @pl.when(has_above)
     def _():
-        for k in range(PIECES):
-            t_paths[k][-1].wait_recv()
-            t_across[k].start()
+        for way, across in zip(t_paths, t_across):
+            way[-1].wait_recv()
+            across.start()
         each(t_across, "wait_recv")
 
     unpack(t_in, t_full)
@@ -333,7 +352,7 @@
         diag_out[...] = t_full[:, mine]
     else:
         diag_out[...] = left - jnp.where(has_above, t_full[...], 0.0)
-    pl.when(has_above)(t_paths[PIECES][-1].wait_recv)
+    pl.when(has_above)(t_paths[-1][-1].wait_recv)
     rhs_out[...] = (
         rhs_ref[...]
         - jnp.where(has_below, from_rhs, 0.0)
@@ -352,10 +371,11 @@
     seqs = rhs.shape[0]
     full = jax.ShapeDtypeStruct((size, size), F32)
     half = jax.ShapeDtypeStruct((size, width), F32)
-    pieces = VMEM((2, PIECES, BLOCK, BLOCK), F32)
+    share = VMEM((PACKED, BLOCK), F32)
+    shares = VMEM((2, PACKED, BLOCK), F32)
     vectors = VMEM((seqs, size), F32)
-    relays = [VMEM((PIECES, BLOCK, BLOCK), F32)] * 2 + [vectors] * 2
-    copies = 4 * PIECES + 3 + (2 * PIECES + 2) * (stride > 1)
+    relays = [share, share, vectors, vectors]
+    copies = 4 * len(CHUNKS) + 3 + (2 * len(CHUNKS) + 2) * (stride > 1)
     return pl.pallas_call(
         functools.partial(level_kernel, stride, last),
         out_shape=(half if last else full, jax.ShapeDtypeStruct((seqs, size), F32), full),
@@ -363,10 +383,12 @@
         out_specs=[pl.BlockSpec(memory_space=VMEM)] * 3,
         scratch_shapes=[
             VMEM((size, size), F32),
-            pieces,
+            share,
+            shares,
             VMEM((size, size), F32),
             VMEM((width + seqs, size), F32),
-            pieces,
+            share,
+            shares,
             VMEM((size, size), F32),
             vectors,
             vectors,

time: 83.5 us -> 79.1 us (0.947)
  Pallas kernels: 76.1 us -> 71.7 us
    pallas_call x2, Pallas kernels: 59.4 us -> 55.1 us  [level(): pl.pallas_call(functools.partial(level_kernel, stride, last), out_shape=(...]
  transfers between devices with their start and end apart: 2 -> 2, of which waited for: 0 -> 0; matrix products, arithmetic and copies ran while one was open for 0% -> 0% of each run, Pallas kernels for 89% -> 88%
where the time goes in v2:
time: 79.1 us; the launch traced here: 78.9 us
  Pallas kernels  71.7 us (91%)
  starting transfers between devices  5.32 us (7%)
  local copies, waits for them, and re-layouts  1.05 us (1%)
    pallas_call x2, Pallas kernels, level(): pl.pallas_call(functools.partial(level_kernel, stride, last), out_shape=(...  55.1 us
    pallas_call x2, Pallas kernels, invert(): pl.pallas_call(invert_kernel, out_shape=jax.ShapeDtypeStruct((size, size)...  11.9 us
    ppermute x2, starting transfers between devices, passed_up(): lax.ppermute(array, 'tm', [(i, i + stride) for i in range(length - stride)])  5.32 us
    pallas_call x1, Pallas kernels, join(): pl.pallas_call(join_kernel, out_shape=jax.ShapeDtypeStruct((size, 2 * wid...  2.64 us
  transfers between devices with their start and end apart: 2, of which 0 were waited for; matrix products, arithmetic and copies ran while one was open for 0% of the time, Pallas kernels for 88%

profile of v2, /device:TPU:256, one launch (start us, length us, event | category | flops | bytes accessed | tf_op | source)
XLA Modules:
  0.0 78.9 jit_solution(5468910117543466270)
XLA Ops:
  0.6 3.4 %collective-permute-start = (f32[512,256]{1,0:T(8,128)}, f32[512,256]{1,0:T(8,128)S(1)}, u32[]{:S(2)}, u32[]{:S(2)}) collective-permute-start(f32[512,256]{1,0:T(8,128)} %bitcast.11), channel_id=1, source_target_pairs={{0,2},{2,4},{4,6},{6,8},{8,10},{10,12},{12,14},{14,16},{16,18},{18... | collective-permute-start | bytes 1572872 | tf_op jit(solution)/shard_map/ppermute | solution.py:441
  4.0 0.0 copy-start
  4.0 1.0 %copy-done = f32[1,512,256]{2,1,0:T(8,128)S(1)} copy-done((f32[1,512,256]{2,1,0:T(8,128)S(1)}, f32[1,512,256]{2,1,0:T(8,128)}, u32[]{:S(2)}) %copy-start) | copy-done | bytes 524312
  5.1 2.6 %join_halves.1.d_ref.diag_ref = f32[512,512]{1,0:T(8,128)S(1)} custom-call(f32[512,256]{1,0:T(8,128)S(1)} %bitcast.10), custom_call_target="tpu_custom_call" | custom-call | tf_op jit(solution)/shard_map/join_halves/pallas_call | solution.py:80
  7.7 0.0 copy-start.1
  7.7 0.0 copy-start.2
  7.8 5.9 %invert_block.2.p_ref = f32[512,512]{1,0:T(8,128)S(1)} custom-call(f32[512,512]{1,0:T(8,128)S(1)} %join_halves.1.d_ref.diag_ref), custom_call_target="tpu_custom_call" | custom-call | flops 3221225472 | bytes 2097152 | tf_op jit(solution)/shard_map/invert_block/pallas_call | solution.py:174
  13.6 0.0 copy-done.1
  13.6 0.0 copy-done.2
  13.6 20.7 %level_1.1 = (f32[512,512]{1,0:T(8,128)S(1)}, f32[64,512]{1,0:T(8,128)S(1)}, f32[512,512]{1,0:T(8,128)S(1)}) custom-call(f32[512,512]{1,0:T(8,128)S(1)} %invert_block.2.p_ref, f32[512,256]{1,0:T(8,128)S(1)} %bitcast.12, f32[512,512]{1,0:T(8,128)S(1)} %join_halves.1.d_ref.diag_ref, f32[64,512]{1,0:T(8,128)S(1)} %bitcast.13), custom_call_target="tpu_custom_call" | custom-call | tf_op jit(solution)/shard_map/level_1/pallas_call | solution.py:379
  34.4 0.0 collective-permute-done.low_prev_ref
  34.4 0.6 couple.1.low_ref
  35.0 1.9 %collective-permute-start.1 = (f32[512,256]{1,0:T(8,128)S(1)}, f32[512,256]{1,0:T(8,128)S(1)}, u32[]{:S(2)}, u32[]{:S(2)}) collective-permute-start(f32[512,256]{1,0:T(8,128)S(1)} %couple.1.low_ref), channel_id=1, source_target_pairs={{0,4},{2,6},{4,8},{6,10},{8,12},{10,14},{12,16},{14,18},{16,20},{1... | collective-permute-start | bytes 1572872 | tf_op jit(solution)/shard_map/ppermute | solution.py:441
  36.9 6.0 %invert_block.3.p_ref = f32[512,512]{1,0:T(8,128)S(1)} custom-call(f32[512,512]{1,0:T(8,128)S(1)} %get-tuple-element.12.d_ref.diag_ref), custom_call_target="tpu_custom_call" | custom-call | flops 3221225472 | bytes 2097152 | tf_op jit(solution)/shard_map/invert_block/pallas_call | solution.py:174
  42.9 34.3 %level_2.1 = (f32[512,256]{1,0:T(8,128)S(1)}, f32[64,512]{1,0:T(8,128)S(1)}, f32[512,512]{1,0:T(8,128)S(1)}) custom-call(f32[512,512]{1,0:T(8,128)S(1)} %invert_block.3.p_ref, f32[512,256]{1,0:T(8,128)S(1)} %couple.1.low_ref, f32[512,512]{1,0:T(8,128)S(1)} %get-tuple-element.12.d_ref.diag_ref, f32[64,512]{1,0:T(8,128)S(1)} %get-tuple-element.14.rhs_ref), custom_call_target="tpu_custom_call" | custom-call | tf_op jit(solution)/shard_map/level_2/pallas_call | solution.py:379
  77.3 0.0 collective-permute-done.1.low_prev_ref
  77.3 1.6 %finish.1 = (f32[512,256]{1,0:T(8,128)}, f32[512,256]{1,0:T(8,128)}, f32[64,512]{1,0:T(8,128)}) custom-call(f32[512,512]{1,0:T(8,128)S(1)} %get-tuple-element.15.carried_ref, f32[512,256]{1,0:T(8,128)S(1)} %collective-permute-done.1.low_prev_ref, f32[512,256]{1,0:T(8,128)S(1)} %get-tuple-element.16.diag_ref, f32[64,512]{1,0:T(8,128)S(1)} %get-tuple-element.17.rhs_ref), custom_call_target="tpu_custom_call" | custom-call | tf_op jit(solution)/shard_map/finish/pallas_call | solution.py:429
Async XLA Ops:
  0.6 33.7 %collective-permute-start = (f32[512,256]{1,0:T(8,128)}, f32[512,256]{1,0:T(8,128)S(1)}, u32[]{:S(2)}, u32[]{:S(2)}) collective-permute-start(f32[512,256]{1,0:T(8,128)} %bitcast.11), channel_id=1, source_target_pairs={{0,2},{2,4},{4,6},{6,8},{8,10},{10,12},{12,14},{14,16},{16,18},{18... | collective-permute-start | bytes 1572872 | tf_op jit(solution)/shard_map/ppermute | solution.py:441
  4.0 1.0 %copy-start = (f32[1,512,256]{2,1,0:T(8,128)S(1)}, f32[1,512,256]{2,1,0:T(8,128)}, u32[]{:S(2)}) copy-start(f32[1,512,256]{2,1,0:T(8,128)} %param.3) | copy-start | bytes 1572868
  7.7 5.9 %copy-start.1 = (f32[1,512,256]{2,1,0:T(8,128)S(1)}, f32[1,512,256]{2,1,0:T(8,128)}, u32[]{:S(2)}) copy-start(f32[1,512,256]{2,1,0:T(8,128)} %param.4) | copy-start | bytes 1572868
  7.7 5.9 %copy-start.2 = (f32[1,512,64]{1,2,0:T(8,128)S(1)}, f32[1,512,64]{1,2,0:T(8,128)}, u32[]{:S(2)}) copy-start(f32[1,512,64]{1,2,0:T(8,128)} %param.5) | copy-start | bytes 393220
  35.0 42.3 %collective-permute-start.1 = (f32[512,256]{1,0:T(8,128)S(1)}, f32[512,256]{1,0:T(8,128)S(1)}, u32[]{:S(2)}, u32[]{:S(2)}) collective-permute-start(f32[512,256]{1,0:T(8,128)S(1)} %couple.1.low_ref), channel_id=1, source_target_pairs={{0,4},{2,6},{4,8},{6,10},{8,12},{10,14},{12,16},{14,18},{16,20},{1... | collective-permute-start | bytes 1572872 | tf_op jit(solution)/shard_map/ppermute | solution.py:441

commit v3 on v2

--- a/solution.py
+++ b/solution.py
@@ -17,7 +17,7 @@
 NT = (((1,), (1,)), ((), ()))
 TN = (((0,), (0,)), ((), ()))
 
-TOLERANCE = 6e-5
+TOLERANCE = 5e-5
 MAX_STEPS = 20
 
 
@@ -133,7 +133,8 @@
         resid = eye - (dot1(a_high[...], x) + dot1(a_low[...], x))
         resid_high = resid.astype(BF16)
         second = dot1(resid_high, resid_high)
-        bound = jnp.sum(resid * resid) * jnp.sum(second * second)
+        bound = jnp.sum(second * second)
+        bound = bound * jnp.sqrt(bound)
         change = halves(resid + second)
         new = x.astype(F32) + (dot1(x, change[0]) + dot1(x, change[1]))
         x_ref[...] = new.astype(BF16)
@@ -305,43 +306,55 @@
         for one in copies:
             getattr(one, call)()
 
+    def pass_on(ways):
+        @pl.when(between)
+        def _():
+            for way in ways:
+                way[0].wait_recv()
+                way[1].start()
+
+    *p_parts, rhs_path = p_paths
+    *t_parts, t_rhs_path = t_paths
     low_across.start()
-    pl.when(has_up)(lambda: each([way[0] for way in p_paths], "start"))
+    pl.when(has_up)(lambda: each([way[0] for way in p_parts], "start"))
     own = halves(jnp.concatenate([low_ref[...].T, rhs_ref[...]], axis=0))
     own = halves(dot3(own, halves(p_ref[...])))
     low_across.wait()
     low = halves(low_full[...])
     t_own[...] = dot3(own, low)
     pack(t_own, 0, core, t_out)
-    pl.when(has_down)(lambda: each([way[0] for way in t_paths], "start"))
-
+    pl.when(has_down)(lambda: each([way[0] for way in t_parts], "start"))
     if relay:
-
-        @pl.when(between)
-        def _():
-            for way in p_paths[:2] + t_paths[:1] + p_paths[2:] + t_paths[1:]:
-                way[0].wait_recv()
-                way[1].start()
+        pass_on(p_parts)
+        pl.when(has_up)(rhs_path[0].start)
+        pass_on(t_parts)
+        pl.when(has_down)(t_rhs_path[0].start)
+        pass_on([rhs_path])
 
     @pl.when(has_below)
     def _():
-        for way, across in zip(p_paths, p_across):
+        for way, across in zip(p_parts, p_across):
             way[-1].wait_recv()
             across.start()
         each(p_across, "wait_recv")
 
+    if not relay:
+        pl.when(has_up)(rhs_path[0].start)
+        pl.when(has_down)(t_rhs_path[0].start)
     unpack(p_in, p_full)
     carried = dot3(low, halves(p_full[...]))
     carried_out[...] = carried
     carried = halves(carried)
     from_diag = dot3(carried, low, NT)
     left = diag_ref[...] - jnp.where(has_below, from_diag, 0.0)
-    pl.when(has_below)(p_paths[-1][-1].wait_recv)
+    if relay:
+        pass_on([t_rhs_path])
+    pl.when(has_below)(rhs_path[-1].wait_recv)
     from_rhs = dot3(halves(rhs_in[...]), carried, NT)
 
     @pl.when(has_above)
     def _():
-        for way, across in zip(t_paths, t_across):
+        for way, across in zip(t_parts, t_across):
             way[-1].wait_recv()
             across.start()
         each(t_across, "wait_recv")
@@ -352,7 +365,7 @@
         diag_out[...] = t_full[:, mine]
     else:
         diag_out[...] = left - jnp.where(has_above, t_full[...], 0.0)
-    pl.when(has_above)(t_paths[-1][-1].wait_recv)
+    pl.when(has_above)(t_rhs_path[-1].wait_recv)
     rhs_out[...] = (
         rhs_ref[...]
         - jnp.where(has_below, from_rhs, 0.0)

time: 79.1 us -> 84.2 us (1.064)
  the two profiles are of different devices: /device:TPU:256 before, /device:TPU:255 now
where the time goes in v3:
time: 84.2 us; the launch traced here: 83.9 us
  Pallas kernels  72.6 us (86%)
  starting transfers between devices  9.49 us (11%)
  local copies, waits for them, and re-layouts  1.05 us (1%)
    pallas_call x2, Pallas kernels, level(): pl.pallas_call(functools.partial(level_kernel, stride, last), out_shape=(...  55.3 us
    pallas_call x2, Pallas kernels, invert(): pl.pallas_call(invert_kernel, out_shape=jax.ShapeDtypeStruct((size, size)...  12 us
    ppermute x2, starting transfers between devices, passed_up(): lax.ppermute(array, 'tm', [(i, i + stride) for i in range(length - stride)])  9.49 us
    pallas_call x1, Pallas kernels, join(): pl.pallas_call(join_kernel, out_shape=jax.ShapeDtypeStruct((size, 2 * wid...  3.22 us
  transfers between devices with their start and end apart: 2, of which 0 were waited for; matrix products, arithmetic and copies ran while one was open for 0% of the time, Pallas kernels for 84%

profile of v3, /device:TPU:255, one launch (start us, length us, event | category | flops | bytes accessed | tf_op | source)
XLA Modules:
  0.0 83.9 jit_solution(3656221821162445735)
XLA Ops:
  0.6 4.3 %collective-permute-start = (f32[512,256]{1,0:T(8,128)}, f32[512,256]{1,0:T(8,128)S(1)}, u32[]{:S(2)}, u32[]{:S(2)}) collective-permute-start(f32[512,256]{1,0:T(8,128)} %bitcast.11), channel_id=1, source_target_pairs={{0,2},{2,4},{4,6},{6,8},{8,10},{10,12},{12,14},{14,16},{16,18},{18... | collective-permute-start | bytes 1572872 | tf_op jit(solution)/shard_map/ppermute | solution.py:454
  5.0 0.0 copy-start
  5.0 1.0 %copy-done = f32[1,512,256]{2,1,0:T(8,128)S(1)} copy-done((f32[1,512,256]{2,1,0:T(8,128)S(1)}, f32[1,512,256]{2,1,0:T(8,128)}, u32[]{:S(2)}) %copy-start) | copy-done | bytes 524312
  6.0 3.2 %join_halves.1.d_ref.diag_ref = f32[512,512]{1,0:T(8,128)S(1)} custom-call(f32[512,256]{1,0:T(8,128)S(1)} %bitcast.10), custom_call_target="tpu_custom_call" | custom-call | tf_op jit(solution)/shard_map/join_halves/pallas_call | solution.py:80
  9.2 0.0 copy-start.1
  9.3 0.0 copy-start.2
  9.3 5.9 %invert_block.2.p_ref = f32[512,512]{1,0:T(8,128)S(1)} custom-call(f32[512,512]{1,0:T(8,128)S(1)} %join_halves.1.d_ref.diag_ref), custom_call_target="tpu_custom_call" | custom-call | flops 3221225472 | bytes 2097152 | tf_op jit(solution)/shard_map/invert_block/pallas_call | solution.py:175
  15.2 0.0 copy-done.1
  15.2 0.0 copy-done.2
  15.2 20.5 %level_1.1 = (f32[512,512]{1,0:T(8,128)S(1)}, f32[64,512]{1,0:T(8,128)S(1)}, f32[512,512]{1,0:T(8,128)S(1)}) custom-call(f32[512,512]{1,0:T(8,128)S(1)} %invert_block.2.p_ref, f32[512,256]{1,0:T(8,128)S(1)} %bitcast.12, f32[512,512]{1,0:T(8,128)S(1)} %join_halves.1.d_ref.diag_ref, f32[64,512]{1,0:T(8,128)S(1)} %bitcast.13), custom_call_target="tpu_custom_call" | custom-call | tf_op jit(solution)/shard_map/level_1/pallas_call | solution.py:392
  35.7 0.0 collective-permute-done.low_prev_ref
  35.7 0.6 couple.1.low_ref
  36.3 5.2 %collective-permute-start.1 = (f32[512,256]{1,0:T(8,128)S(1)}, f32[512,256]{1,0:T(8,128)S(1)}, u32[]{:S(2)}, u32[]{:S(2)}) collective-permute-start(f32[512,256]{1,0:T(8,128)S(1)} %couple.1.low_ref), channel_id=1, source_target_pairs={{0,4},{2,6},{4,8},{6,10},{8,12},{10,14},{12,16},{14,18},{16,20},{1... | collective-permute-start | bytes 1572872 | tf_op jit(solution)/shard_map/ppermute | solution.py:454
  41.5 6.1 %invert_block.3.p_ref = f32[512,512]{1,0:T(8,128)S(1)} custom-call(f32[512,512]{1,0:T(8,128)S(1)} %get-tuple-element.12.d_ref.diag_ref), custom_call_target="tpu_custom_call" | custom-call | flops 3221225472 | bytes 2097152 | tf_op jit(solution)/shard_map/invert_block/pallas_call | solution.py:175
  47.5 34.8 %level_2.1 = (f32[512,256]{1,0:T(8,128)S(1)}, f32[64,512]{1,0:T(8,128)S(1)}, f32[512,512]{1,0:T(8,128)S(1)}) custom-call(f32[512,512]{1,0:T(8,128)S(1)} %invert_block.3.p_ref, f32[512,256]{1,0:T(8,128)S(1)} %couple.1.low_ref, f32[512,512]{1,0:T(8,128)S(1)} %get-tuple-element.12.d_ref.diag_ref, f32[64,512]{1,0:T(8,128)S(1)} %get-tuple-element.14.rhs_ref), custom_call_target="tpu_custom_call" | custom-call | tf_op jit(solution)/shard_map/level_2/pallas_call | solution.py:392
  82.3 0.0 collective-permute-done.1.low_prev_ref
  82.3 1.6 %finish.1 = (f32[512,256]{1,0:T(8,128)}, f32[512,256]{1,0:T(8,128)}, f32[64,512]{1,0:T(8,128)}) custom-call(f32[512,512]{1,0:T(8,128)S(1)} %get-tuple-element.15.carried_ref, f32[512,256]{1,0:T(8,128)S(1)} %collective-permute-done.1.low_prev_ref, f32[512,256]{1,0:T(8,128)S(1)} %get-tuple-element.16.diag_ref, f32[64,512]{1,0:T(8,128)S(1)} %get-tuple-element.17.rhs_ref), custom_call_target="tpu_custom_call" | custom-call | tf_op jit(solution)/shard_map/finish/pallas_call | solution.py:442
Async XLA Ops:
  0.6 35.1 %collective-permute-start = (f32[512,256]{1,0:T(8,128)}, f32[512,256]{1,0:T(8,128)S(1)}, u32[]{:S(2)}, u32[]{:S(2)}) collective-permute-start(f32[512,256]{1,0:T(8,128)} %bitcast.11), channel_id=1, source_target_pairs={{0,2},{2,4},{4,6},{6,8},{8,10},{10,12},{12,14},{14,16},{16,18},{18... | collective-permute-start | bytes 1572872 | tf_op jit(solution)/shard_map/ppermute | solution.py:454
  5.0 1.0 %copy-start = (f32[1,512,256]{2,1,0:T(8,128)S(1)}, f32[1,512,256]{2,1,0:T(8,128)}, u32[]{:S(2)}) copy-start(f32[1,512,256]{2,1,0:T(8,128)} %param.3) | copy-start | bytes 1572868
  9.2 5.9 %copy-start.1 = (f32[1,512,256]{2,1,0:T(8,128)S(1)}, f32[1,512,256]{2,1,0:T(8,128)}, u32[]{:S(2)}) copy-start(f32[1,512,256]{2,1,0:T(8,128)} %param.4) | copy-start | bytes 1572868
  9.3 5.9 %copy-start.2 = (f32[1,512,64]{1,2,0:T(8,128)S(1)}, f32[1,512,64]{1,2,0:T(8,128)}, u32[]{:S(2)}) copy-start(f32[1,512,64]{1,2,0:T(8,128)} %param.5) | copy-start | bytes 393220
  36.3 46.0 %collective-permute-start.1 = (f32[512,256]{1,0:T(8,128)S(1)}, f32[512,256]{1,0:T(8,128)S(1)}, u32[]{:S(2)}, u32[]{:S(2)}) collective-permute-start(f32[512,256]{1,0:T(8,128)S(1)} %couple.1.low_ref), channel_id=1, source_target_pairs={{0,4},{2,6},{4,8},{6,10},{8,12},{10,14},{12,16},{14,18},{16,20},{1... | collective-permute-start | bytes 1572872 | tf_op jit(solution)/shard_map/ppermute | solution.py:454

commit v4 on v2

--- a/solution.py
+++ b/solution.py
@@ -17,7 +17,7 @@
 NT = (((1,), (1,)), ((), ()))
 TN = (((0,), (0,)), ((), ()))
 
-TOLERANCE = 6e-5
+TOLERANCE = 5e-5
 MAX_STEPS = 20
 
 
@@ -133,7 +133,8 @@
         resid = eye - (dot1(a_high[...], x) + dot1(a_low[...], x))
         resid_high = resid.astype(BF16)
         second = dot1(resid_high, resid_high)
-        bound = jnp.sum(resid * resid) * jnp.sum(second * second)
+        bound = jnp.sum(second * second)
+        bound = bound * jnp.sqrt(bound)
         change = halves(resid + second)
         new = x.astype(F32) + (dot1(x, change[0]) + dot1(x, change[1]))
         x_ref[...] = new.astype(BF16)
@@ -192,26 +193,30 @@
 
 BLOCK = 128
 PACKED = 4 * BLOCK + 8
-CHUNKS = ((0, 2 * BLOCK), (2 * BLOCK, 2 * BLOCK + 8))
-
-
-def pack(ref, first_row, core, packed):
-    own, other = 2 * core, 2 - 2 * core
-
-    def block(row, col):
-        row = pl.multiple_of(first_row + row * BLOCK, BLOCK)
-        col = pl.multiple_of(col * BLOCK, BLOCK)
-        return ref[pl.ds(row, BLOCK), pl.ds(col, BLOCK)]
-
-    packed[:BLOCK] = block(0, own + 1)
-    packed[BLOCK : 2 * BLOCK] = block(core, other)
-    packed[2 * BLOCK : 3 * BLOCK] = block(1, other + core)
+NEAR = 2 * BLOCK + 8
+CHUNKS = ((0, NEAR), (NEAR, 2 * BLOCK))
+
+
+def block_at(ref, row, col):
+    row, col = pl.multiple_of(row * BLOCK, BLOCK), pl.multiple_of(col * BLOCK, BLOCK)
+    return ref[pl.ds(row, BLOCK), pl.ds(col, BLOCK)]
+
+
+def pack_near(ref, first, core, packed):
+    own = 2 * core
+    packed[:BLOCK] = block_at(ref, first, own + 1)
     rows = lax.broadcasted_iota(jnp.int32, (BLOCK, BLOCK), 0)
     cols = lax.broadcasted_iota(jnp.int32, (BLOCK, BLOCK), 1)
-    second = block(1, own + 1)
-    packed[3 * BLOCK : 4 * BLOCK] = jnp.where(rows >= cols, block(0, own), second)
+    second = block_at(ref, first + 1, own + 1)
+    packed[BLOCK : 2 * BLOCK] = jnp.where(rows >= cols, block_at(ref, first, own), second)
     diagonal = jnp.sum(jnp.where(rows == cols, second, 0.0), axis=0, keepdims=True)
-    packed[4 * BLOCK :] = jnp.broadcast_to(diagonal, (8, BLOCK))
+    packed[2 * BLOCK : NEAR] = jnp.broadcast_to(diagonal, (8, BLOCK))
+
+
+def pack_far(ref, first, core, packed):
+    other = 2 - 2 * core
+    packed[NEAR : NEAR + BLOCK] = block_at(ref, first + core, other)
+    packed[NEAR + BLOCK :] = block_at(ref, first + 1, other + core)
 
 
 def unpack(shares, full):
@@ -221,13 +226,13 @@
     rows = lax.broadcasted_iota(jnp.int32, (BLOCK, BLOCK), 0)
     cols = lax.broadcasted_iota(jnp.int32, (BLOCK, BLOCK), 1)
     for core, places in enumerate((((0, 1), (0, 2), (1, 2)), ((2, 3), (3, 0), (3, 1)))):
-        for k, (row, col) in enumerate(places):
-            value = shares[core, k * BLOCK : (k + 1) * BLOCK]
+        for at, (row, col) in zip((0, NEAR, NEAR + BLOCK), places):
+            value = shares[core, at : at + BLOCK]
             put(row, col, value)
             put(col, row, value.T)
-        both = shares[core, 3 * BLOCK : 4 * BLOCK]
+        both = shares[core, BLOCK : 2 * BLOCK]
         turned = both.T
-        diagonal = shares[core, 4 * BLOCK : 4 * BLOCK + 1]
+        diagonal = shares[core, 2 * BLOCK : 2 * BLOCK + 1]
         put(2 * core, 2 * core, jnp.where(rows >= cols, both, turned))
         second = jnp.where(rows < cols, both, jnp.where(rows > cols, turned, diagonal))
         put(2 * core + 1, 2 * core + 1, second)
@@ -261,7 +266,8 @@
     pl.when(near_up)(lambda: signal(up))
     pl.when(near_down)(lambda: signal(down))
     low_full[:, mine] = low_ref[...]
-    pack(p_ref, first, core, p_out)
+    pack_near(p_ref, 2 * core, core, p_out)
+    pack_far(p_ref, 2 * core, core, p_out)
     pl.semaphore_wait(
         barrier, 1 + near_up.astype(jnp.int32) + near_down.astype(jnp.int32)
     )
@@ -285,9 +291,10 @@
         return [copy(src, held, device), copy(held, dst, device)]
 
     def packed_paths(out, held, into, device):
+        parts = [pl.ds(at, n) for at, n in CHUNKS]
         return [
-            path(out.at[pl.ds(at, n)], relay and held.at[pl.ds(at, n)], into.at[core, pl.ds(at, n)], device)
-            for at, n in CHUNKS
+            path(out.at[part], relay and held.at[part], into.at[core, part], device)
+            for part in parts
         ]
 
     def packed_across(into):
@@ -309,12 +316,15 @@
     pl.when(has_up)(lambda: each([way[0] for way in p_paths], "start"))
     own = halves(jnp.concatenate([low_ref[...].T, rhs_ref[...]], axis=0))
     own = halves(dot3(own, halves(p_ref[...])))
+    t_own[:, mine] = dot3(own, halves(low_ref[...]))
+    pack_near(t_own, 0, core, t_out)
+    pl.when(has_down)(t_paths[0][0].start)
     low_across.wait()
+    others = pl.ds(pl.multiple_of((1 - core) * width, width), width)
+    t_own[:, others] = dot3(own, halves(low_full[:, others]))
+    pack_far(t_own, 0, core, t_out)
+    pl.when(has_down)(lambda: each([way[0] for way in t_paths[1:]], "start"))
     low = halves(low_full[...])
-    t_own[...] = dot3(own, low)
-    pack(t_own, 0, core, t_out)
-    pl.when(has_down)(lambda: each([way[0] for way in t_paths], "start"))
-
     if relay:
 
         @pl.when(between)

time: 79.1 us -> 79.1 us (level)
  no operation moved by 1% of the time
where the time goes in v4:
time: 79.1 us; the launch traced here: 78.9 us
  Pallas kernels  71.7 us (91%)
  starting transfers between devices  5.32 us (7%)
  local copies, waits for them, and re-layouts  1.05 us (1%)
    pallas_call x2, Pallas kernels, level(): pl.pallas_call(functools.partial(level_kernel, stride, last), out_shape=(...  55 us
    pallas_call x2, Pallas kernels, invert(): pl.pallas_call(invert_kernel, out_shape=jax.ShapeDtypeStruct((size, size)...  12 us
    ppermute x2, starting transfers between devices, passed_up(): lax.ppermute(array, 'tm', [(i, i + stride) for i in range(length - stride)])  5.32 us
    pallas_call x1, Pallas kernels, join(): pl.pallas_call(join_kernel, out_shape=jax.ShapeDtypeStruct((size, 2 * wid...  2.64 us
  transfers between devices with their start and end apart: 2, of which 0 were waited for; matrix products, arithmetic and copies ran while one was open for 0% of the time, Pallas kernels for 88%

profile of v4, /device:TPU:256, one launch (start us, length us, event | category | flops | bytes accessed | tf_op | source)
XLA Modules:
  0.0 78.9 jit_solution(16037484764975467666)
XLA Ops:
  0.6 3.4 %collective-permute-start = (f32[512,256]{1,0:T(8,128)}, f32[512,256]{1,0:T(8,128)S(1)}, u32[]{:S(2)}, u32[]{:S(2)}) collective-permute-start(f32[512,256]{1,0:T(8,128)} %bitcast.11), channel_id=1, source_target_pairs={{0,2},{2,4},{4,6},{6,8},{8,10},{10,12},{12,14},{14,16},{16,18},{18... | collective-permute-start | bytes 1572872 | tf_op jit(solution)/shard_map/ppermute | solution.py:451
  4.0 0.0 copy-start
  4.0 1.0 %copy-done = f32[1,512,256]{2,1,0:T(8,128)S(1)} copy-done((f32[1,512,256]{2,1,0:T(8,128)S(1)}, f32[1,512,256]{2,1,0:T(8,128)}, u32[]{:S(2)}) %copy-start) | copy-done | bytes 524312
  5.1 2.6 %join_halves.1.d_ref.diag_ref = f32[512,512]{1,0:T(8,128)S(1)} custom-call(f32[512,256]{1,0:T(8,128)S(1)} %bitcast.10), custom_call_target="tpu_custom_call" | custom-call | tf_op jit(solution)/shard_map/join_halves/pallas_call | solution.py:80
  7.7 0.0 copy-start.1
  7.7 0.0 copy-start.2
  7.8 5.9 %invert_block.2.p_ref = f32[512,512]{1,0:T(8,128)S(1)} custom-call(f32[512,512]{1,0:T(8,128)S(1)} %join_halves.1.d_ref.diag_ref), custom_call_target="tpu_custom_call" | custom-call | flops 3221225472 | bytes 2097152 | tf_op jit(solution)/shard_map/invert_block/pallas_call | solution.py:175
  13.7 0.0 copy-done.1
  13.7 0.0 copy-done.2
  13.7 20.7 %level_1.1 = (f32[512,512]{1,0:T(8,128)S(1)}, f32[64,512]{1,0:T(8,128)S(1)}, f32[512,512]{1,0:T(8,128)S(1)}) custom-call(f32[512,512]{1,0:T(8,128)S(1)} %invert_block.2.p_ref, f32[512,256]{1,0:T(8,128)S(1)} %bitcast.12, f32[512,512]{1,0:T(8,128)S(1)} %join_halves.1.d_ref.diag_ref, f32[64,512]{1,0:T(8,128)S(1)} %bitcast.13), custom_call_target="tpu_custom_call" | custom-call | tf_op jit(solution)/shard_map/level_1/pallas_call | solution.py:389
  34.4 0.0 collective-permute-done.low_prev_ref
  34.4 0.6 couple.1.low_ref
  35.0 1.9 %collective-permute-start.1 = (f32[512,256]{1,0:T(8,128)S(1)}, f32[512,256]{1,0:T(8,128)S(1)}, u32[]{:S(2)}, u32[]{:S(2)}) collective-permute-start(f32[512,256]{1,0:T(8,128)S(1)} %couple.1.low_ref), channel_id=1, source_target_pairs={{0,4},{2,6},{4,8},{6,10},{8,12},{10,14},{12,16},{14,18},{16,20},{1... | collective-permute-start | bytes 1572872 | tf_op jit(solution)/shard_map/ppermute | solution.py:451
  36.9 6.1 %invert_block.3.p_ref = f32[512,512]{1,0:T(8,128)S(1)} custom-call(f32[512,512]{1,0:T(8,128)S(1)} %get-tuple-element.12.d_ref.diag_ref), custom_call_target="tpu_custom_call" | custom-call | flops 3221225472 | bytes 2097152 | tf_op jit(solution)/shard_map/invert_block/pallas_call | solution.py:175
  43.0 34.3 %level_2.1 = (f32[512,256]{1,0:T(8,128)S(1)}, f32[64,512]{1,0:T(8,128)S(1)}, f32[512,512]{1,0:T(8,128)S(1)}) custom-call(f32[512,512]{1,0:T(8,128)S(1)} %invert_block.3.p_ref, f32[512,256]{1,0:T(8,128)S(1)} %couple.1.low_ref, f32[512,512]{1,0:T(8,128)S(1)} %get-tuple-element.12.d_ref.diag_ref, f32[64,512]{1,0:T(8,128)S(1)} %get-tuple-element.14.rhs_ref), custom_call_target="tpu_custom_call" | custom-call | tf_op jit(solution)/shard_map/level_2/pallas_call | solution.py:389
  77.3 0.0 collective-permute-done.1.low_prev_ref
  77.3 1.5 %finish.1 = (f32[512,256]{1,0:T(8,128)}, f32[512,256]{1,0:T(8,128)}, f32[64,512]{1,0:T(8,128)}) custom-call(f32[512,512]{1,0:T(8,128)S(1)} %get-tuple-element.15.carried_ref, f32[512,256]{1,0:T(8,128)S(1)} %collective-permute-done.1.low_prev_ref, f32[512,256]{1,0:T(8,128)S(1)} %get-tuple-element.16.diag_ref, f32[64,512]{1,0:T(8,128)S(1)} %get-tuple-element.17.rhs_ref), custom_call_target="tpu_custom_call" | custom-call | tf_op jit(solution)/shard_map/finish/pallas_call | solution.py:439
Async XLA Ops:
  0.6 33.8 %collective-permute-start = (f32[512,256]{1,0:T(8,128)}, f32[512,256]{1,0:T(8,128)S(1)}, u32[]{:S(2)}, u32[]{:S(2)}) collective-permute-start(f32[512,256]{1,0:T(8,128)} %bitcast.11), channel_id=1, source_target_pairs={{0,2},{2,4},{4,6},{6,8},{8,10},{10,12},{12,14},{14,16},{16,18},{18... | collective-permute-start | bytes 1572872 | tf_op jit(solution)/shard_map/ppermute | solution.py:451
  4.0 1.0 %copy-start = (f32[1,512,256]{2,1,0:T(8,128)S(1)}, f32[1,512,256]{2,1,0:T(8,128)}, u32[]{:S(2)}) copy-start(f32[1,512,256]{2,1,0:T(8,128)} %param.3) | copy-start | bytes 1572868
  7.7 5.9 %copy-start.1 = (f32[1,512,256]{2,1,0:T(8,128)S(1)}, f32[1,512,256]{2,1,0:T(8,128)}, u32[]{:S(2)}) copy-start(f32[1,512,256]{2,1,0:T(8,128)} %param.4) | copy-start | bytes 1572868
  7.7 5.9 %copy-start.2 = (f32[1,512,64]{1,2,0:T(8,128)S(1)}, f32[1,512,64]{1,2,0:T(8,128)}, u32[]{:S(2)}) copy-start(f32[1,512,64]{1,2,0:T(8,128)} %param.5) | copy-start | bytes 393220
  35.0 42.3 %collective-permute-start.1 = (f32[512,256]{1,0:T(8,128)S(1)}, f32[512,256]{1,0:T(8,128)S(1)}, u32[]{:S(2)}, u32[]{:S(2)}) collective-permute-start(f32[512,256]{1,0:T(8,128)S(1)} %couple.1.low_ref), channel_id=1, source_target_pairs={{0,4},{2,6},{4,8},{6,10},{8,12},{10,14},{12,16},{14,18},{16,20},{1... | collective-permute-start | bytes 1572872 | tf_op jit(solution)/shard_map/ppermute | solution.py:451

commit v5 on v4

--- a/solution.py
+++ b/solution.py
@@ -32,6 +32,13 @@
 
 def dot3(a, b, dims=NN):
     return dot1(a[0], b[0], dims) + (dot1(a[0], b[1], dims) + dot1(a[1], b[0], dims))
+
+
+RING = 4
+
+
+def row_at(row, turn):
+    return row - row % RING + (row + turn) % RING
 
 
 def neighbours(stride):
@@ -238,11 +245,14 @@
         put(2 * core + 1, 2 * core + 1, second)
 
 
-def level_kernel(
-    stride, last, p_ref, low_ref, diag_ref, rhs_ref, diag_out, rhs_out, carried_out,
-    low_full, p_out, p_in, p_full, t_own, t_out, t_in, t_full, t_rhs_in, rhs_in, *rest,
-):
+def level_kernel(stride, last, *refs):
     relay = stride > 1
+    p_ref, low_ref, diag_ref, rhs_ref, *refs = refs
+    if relay:
+        held_ref, diag_out, rhs_out, carried_out, end_out, *refs = refs
+    else:
+        diag_out, rhs_out, carried_out, *refs = refs
+    low_full, p_out, p_in, p_full, t_own, t_out, t_in, t_full, t_rhs_in, rhs_in, *rest = refs
     if relay:
         p_relay, t_relay, rhs_relay, t_rhs_relay, sems = rest
     else:
@@ -265,12 +275,16 @@
     signal(sibling)
     pl.when(near_up)(lambda: signal(up))
     pl.when(near_down)(lambda: signal(down))
+    waits = 1 + near_up.astype(jnp.int32) + near_down.astype(jnp.int32)
+    if relay:
+        onward = row_at(row, 1) + stride
+        has_onward = onward < length
+        pl.when(has_below)(lambda: signal((row_at(row - stride, RING - 1), core)))
+        waits += has_onward.astype(jnp.int32)
     low_full[:, mine] = low_ref[...]
     pack_near(p_ref, 2 * core, core, p_out)
     pack_far(p_ref, 2 * core, core, p_out)
-    pl.semaphore_wait(
-        barrier, 1 + near_up.astype(jnp.int32) + near_down.astype(jnp.int32)
-    )
+    pl.semaphore_wait(barrier, waits)
 
     used = iter(range(sems.shape[1]))
 
@@ -313,6 +327,9 @@
             getattr(one, call)()
 
     low_across.start()
+    if relay:
+        end_copy = copy(held_ref, end_out, (onward, core))
+        pl.when(has_onward)(end_copy.start)
     pl.when(has_up)(lambda: each([way[0] for way in p_paths], "start"))
     own = halves(jnp.concatenate([low_ref[...].T, rhs_ref[...]], axis=0))
     own = halves(dot3(own, halves(p_ref[...])))
@@ -372,25 +389,31 @@
     pl.when(has_down)(lambda: each([way[0] for way in t_paths], "wait_send"))
     if relay:
         pl.when(between)(lambda: each([way[1] for way in p_paths + t_paths], "wait_send"))
+        pl.when(has_below)(end_copy.wait_recv)
+        pl.when(has_onward)(end_copy.wait_send)
     pl.when(has_below)(lambda: each(p_across, "wait_send"))
     pl.when(has_above)(lambda: each(t_across, "wait_send"))
 
 
-def level(stride, last, p, low_cols, diag, rhs):
+def level(stride, last, p, low_cols, diag, rhs, *held):
     size, width = low_cols.shape
     seqs = rhs.shape[0]
+    relay = stride > 1
     full = jax.ShapeDtypeStruct((size, size), F32)
     half = jax.ShapeDtypeStruct((size, width), F32)
     share = VMEM((PACKED, BLOCK), F32)
     shares = VMEM((2, PACKED, BLOCK), F32)
     vectors = VMEM((seqs, size), F32)
     relays = [share, share, vectors, vectors]
-    copies = 4 * len(CHUNKS) + 3 + (2 * len(CHUNKS) + 2) * (stride > 1)
+    copies = 4 * len(CHUNKS) + 3 + (2 * len(CHUNKS) + 3) * relay
+    out_shape = [half if last else full, jax.ShapeDtypeStruct((seqs, size), F32), full]
+    out_shape += [jax.ShapeDtypeStruct(part.shape, F32) for part in held]
+    in_vmem = pl.BlockSpec(memory_space=VMEM)
     return pl.pallas_call(
         functools.partial(level_kernel, stride, last),
-        out_shape=(half if last else full, jax.ShapeDtypeStruct((seqs, size), F32), full),
-        in_specs=[pl.BlockSpec(memory_space=VMEM)] * 4,
-        out_specs=[pl.BlockSpec(memory_space=VMEM)] * 3,
+        out_shape=out_shape,
+        in_specs=[in_vmem] * (4 + len(held)),
+        out_specs=[in_vmem] * len(out_shape),
         scratch_shapes=[
             VMEM((size, size), F32),
             share,
@@ -402,48 +425,66 @@
             VMEM((size, size), F32),
             vectors,
             vectors,
-            *(relays if stride > 1 else ()),
+            *(relays if relay else ()),
             pltpu.SemaphoreType.DMA((2, copies)),
         ],
         compiler_params=pltpu.CompilerParams(
             collective_id=stride, has_side_effects=True, vmem_limit_bytes=VMEM_LIMIT
         ),
         name="level_%d" % stride,
-    )(p, low_cols, diag, rhs)
-
-
-def couple_kernel(stride, carried_ref, low_prev_ref, low_out):
-    product = dot3(halves(carried_ref[...]), halves(low_prev_ref[...]))
-    low_out[...] = jnp.where(lax.axis_index("tm") >= 2 * stride, -product, 0.0)
+    )(p, low_cols, diag, rhs, *held)
+
+
+def coupling(stride, carried_ref, *low_prev):
+    carried = halves(carried_ref[...])
+    total, at = 0.0, 0
+    for part in low_prev:
+        rows = part.shape[0]
+        total += dot3([half[:, at : at + rows] for half in carried], halves(part[...]))
+        at += rows
+    return jnp.where(lax.axis_index("tm") >= 2 * stride, -total, 0.0)
+
+
+def couple_kernel(stride, carried_ref, low_prev_ref, low_out, top_out, end_out):
+    low = coupling(stride, carried_ref, low_prev_ref)
+    cut = top_out.shape[0]
+    low_out[...] = low
+    top_out[...] = low[:cut]
+    end_out[...] = low[cut:]
 
 
 def couple(stride, carried, low_prev):
+    size, width = low_prev.shape
+    part = jax.ShapeDtypeStruct((size // 2, width), F32)
+    in_vmem = pl.BlockSpec(memory_space=VMEM)
     return pl.pallas_call(
         functools.partial(couple_kernel, stride),
-        out_shape=jax.ShapeDtypeStruct(low_prev.shape, F32),
-        in_specs=[pl.BlockSpec(memory_space=VMEM)] * 2,
-        out_specs=pl.BlockSpec(memory_space=VMEM),
+        out_shape=(jax.ShapeDtypeStruct((size, width), F32), part, part),
+        in_specs=[in_vmem] * 2,
+        out_specs=[in_vmem] * 3,
         compiler_params=pltpu.CompilerParams(vmem_limit_bytes=VMEM_LIMIT),
         name="couple",
     )(carried, low_prev)
 
 
-def finish_kernel(stride, carried_ref, low_prev_ref, diag_ref, rhs_ref, diag_out, low_out, rhs_out):
-    couple_kernel(stride, carried_ref, low_prev_ref, low_out)
+def finish_kernel(
+    stride, carried_ref, top_ref, end_ref, diag_ref, rhs_ref, diag_out, low_out, rhs_out
+):
+    low_out[...] = coupling(stride, carried_ref, top_ref, end_ref)
     diag_out[...] = diag_ref[...]
     rhs_out[...] = rhs_ref[...]
 
 
-def finish(stride, carried, low_prev, diag, rhs):
+def finish(stride, carried, top, end, diag, rhs):
     half = jax.ShapeDtypeStruct(diag.shape, F32)
     return pl.pallas_call(
         functools.partial(finish_kernel, stride),
         out_shape=(half, half, jax.ShapeDtypeStruct(rhs.shape, F32)),
-        in_specs=[pl.BlockSpec(memory_space=VMEM)] * 4,
+        in_specs=[pl.BlockSpec(memory_space=VMEM)] * 5,
         out_specs=[pl.BlockSpec(memory_space=VMEM)] * 3,
         compiler_params=pltpu.CompilerParams(vmem_limit_bytes=VMEM_LIMIT),
         name="finish",
-    )(carried, low_prev, diag, rhs)
+    )(carried, top, end, diag, rhs)
 
 
 def passed_up(array, stride):
@@ -451,16 +492,23 @@
     return lax.ppermute(array, "tm", [(i, i + stride) for i in range(length - stride)])
 
 
+def passed_west(array, stride):
+    length = lax.axis_size("tm")
+    pairs = [(i, row_at(i, RING - 1)) for i in range(length - stride)]
+    return lax.ppermute(array, "tm", pairs)
+
+
 def per_device(diagonal, lower, rhs):
-    low_cols, rhs_rows = lower[0], rhs[0].T
-    low_prev = passed_up(low_cols, 1)
+    low, rhs_rows = lower[0], rhs[0].T
+    low_prev = passed_up(low, 1)
     diag = join(diagonal[0])
-    diag, rhs_rows, carried = level(1, False, invert(diag), low_cols, diag, rhs_rows)
-    low_cols = couple(1, carried, low_prev)
-    low_prev = passed_up(low_cols, 2)
-    diag, rhs_rows, carried = level(2, True, invert(diag), low_cols, diag, rhs_rows)
-    diag, low_cols, rhs_rows = finish(2, carried, low_prev, diag, rhs_rows)
-    return diag[None], low_cols[None], rhs_rows.T[None]
+    diag, rhs_rows, carried = level(1, False, invert(diag), low, diag, rhs_rows)
+    low, low_top, low_end = couple(1, carried, low_prev)
+    held = passed_west(low_end, 2)
+    top = passed_up(low_top, 2)
+    diag, rhs_rows, carried, end = level(2, True, invert(diag), low, diag, rhs_rows, held)
+    diag, low, rhs_rows = finish(2, carried, top, end, diag, rhs_rows)
+    return diag[None], low[None], rhs_rows.T[None]
 
 
 def solution(mesh):

time: 79.1 us -> 84.4 us (1.067)
  starting transfers between devices: 5.32 us -> 9.81 us
    ppermute x2, starting transfers between devices: 5.32 us -> 7.89 us  [passed_up(): lax.ppermute(array, 'tm', [(i, i + stride) for i in range(length - stride)])]
    ppermute x0 -> x1, starting transfers between devices: none -> 1.92 us  [passed_west(): return lax.ppermute(array, 'tm', pairs)]
  transfers between devices with their start and end apart: 2 -> 3, of which waited for: 0 -> 0; matrix products, arithmetic and copies ran while one was open for 0% -> 0% of each run, Pallas kernels for 88% -> 84%
where the time goes in v5:
time: 84.4 us; the launch traced here: 84.1 us
  Pallas kernels  72.5 us (86%)
  starting transfers between devices  9.81 us (12%)
  local copies, waits for them, and re-layouts  1.05 us (1%)
    pallas_call x2, Pallas kernels, level(): pl.pallas_call(functools.partial(level_kernel, stride, last), out_shape=o...  55.7 us
    pallas_call x2, Pallas kernels, invert(): pl.pallas_call(invert_kernel, out_shape=jax.ShapeDtypeStruct((size, size)...  12 us
    ppermute x2, starting transfers between devices, passed_up(): lax.ppermute(array, 'tm', [(i, i + stride) for i in range(length - stride)])  7.89 us
    pallas_call x1, Pallas kernels, join(): pl.pallas_call(join_kernel, out_shape=jax.ShapeDtypeStruct((size, 2 * wid...  2.64 us
    ppermute x1, starting transfers between devices, passed_west(): return lax.ppermute(array, 'tm', pairs)  1.92 us
  transfers between devices with their start and end apart: 3, of which 0 were waited for; matrix products, arithmetic and copies ran while one was open for 0% of the time, Pallas kernels for 84%

profile of v5, /device:TPU:256, one launch (start us, length us, event | category | flops | bytes accessed | tf_op | source)
XLA Modules:
  0.0 84.1 jit_solution(1406892973836718946)
XLA Ops:
  0.6 3.4 %collective-permute-start = (f32[512,256]{1,0:T(8,128)}, f32[512,256]{1,0:T(8,128)S(1)}, u32[]{:S(2)}, u32[]{:S(2)}) collective-permute-start(f32[512,256]{1,0:T(8,128)} %bitcast.11), channel_id=1, source_target_pairs={{0,2},{2,4},{4,6},{6,8},{8,10},{10,12},{12,14},{14,16},{16,18},{18... | collective-permute-start | bytes 1572872 | tf_op jit(solution)/shard_map/ppermute | solution.py:492
  4.0 0.0 copy-start
  4.0 1.0 %copy-done = f32[1,512,256]{2,1,0:T(8,128)S(1)} copy-done((f32[1,512,256]{2,1,0:T(8,128)S(1)}, f32[1,512,256]{2,1,0:T(8,128)}, u32[]{:S(2)}) %copy-start) | copy-done | bytes 524312
  5.1 2.6 %join_halves.1.d_ref.refs_2_ = f32[512,512]{1,0:T(8,128)S(1)} custom-call(f32[512,256]{1,0:T(8,128)S(1)} %bitcast.10), custom_call_target="tpu_custom_call" | custom-call | tf_op jit(solution)/shard_map/join_halves/pallas_call | solution.py:87
  7.7 0.0 copy-start.1
  7.7 0.0 copy-start.2
  7.8 5.9 %invert_block.2.refs_0_ = f32[512,512]{1,0:T(8,128)S(1)} custom-call(f32[512,512]{1,0:T(8,128)S(1)} %join_halves.1.d_ref.refs_2_), custom_call_target="tpu_custom_call" | custom-call | flops 3221225472 | bytes 2097152 | tf_op jit(solution)/shard_map/invert_block/pallas_call | solution.py:182
  13.7 0.0 copy-done.1
  13.7 0.0 copy-done.2
  13.7 20.7 %level_1.1 = (f32[512,512]{1,0:T(8,128)S(1)}, f32[64,512]{1,0:T(8,128)S(1)}, f32[512,512]{1,0:T(8,128)S(1)}) custom-call(f32[512,512]{1,0:T(8,128)S(1)} %invert_block.2.refs_0_, f32[512,256]{1,0:T(8,128)S(1)} %bitcast.12, f32[512,512]{1,0:T(8,128)S(1)} %join_halves.1.d_ref.refs_2_, f32[64,512]{1,0:T(8,128)S(1)} %bitcast.13), custom_call_target="tpu_custom_call" | custom-call | tf_op jit(solution)/shard_map/level_1/pallas_call | solution.py:412
  34.4 0.0 collective-permute-done.low_prev_ref
  34.4 0.6 couple.1
  35.0 1.9 %collective-permute-start.1 = (f32[256,256]{1,0:T(8,128)S(1)}, f32[256,256]{1,0:T(8,128)S(1)}, u32[]{:S(2)}, u32[]{:S(2)}) collective-permute-start(f32[256,256]{1,0:T(8,128)S(1)} %get-tuple-element.20), channel_id=1, source_target_pairs={{0,6},{2,0},{4,2},{6,4},{8,14},{10,8},{12,10},{14,12},{16,22},{18,... | collective-permute-start | bytes 786440 | tf_op jit(solution)/shard_map/ppermute | solution.py:498
  36.9 4.5 %collective-permute-start.2 = (f32[256,256]{1,0:T(8,128)S(1)}, f32[256,256]{1,0:T(8,128)S(1)}, u32[]{:S(2)}, u32[]{:S(2)}) collective-permute-start(f32[256,256]{1,0:T(8,128)S(1)} %get-tuple-element.22), channel_id=1, source_target_pairs={{0,4},{2,6},{4,8},{6,10},{8,12},{10,14},{12,16},{14,18},{16,20},{1... | collective-permute-start | bytes 786440 | tf_op jit(solution)/shard_map/ppermute | solution.py:492
  41.4 6.1 %invert_block.3.refs_0_ = f32[512,512]{1,0:T(8,128)S(1)} custom-call(f32[512,512]{1,0:T(8,128)S(1)} %get-tuple-element.16.d_ref.refs_2_), custom_call_target="tpu_custom_call" | custom-call | flops 3221225472 | bytes 2097152 | tf_op jit(solution)/shard_map/invert_block/pallas_call | solution.py:182
  47.5 0.0 collective-permute-done.1.refs_4_
  47.5 35.0 %level_2.1 = (f32[512,256]{1,0:T(8,128)S(1)}, f32[64,512]{1,0:T(8,128)S(1)}, f32[512,512]{1,0:T(8,128)S(1)}, f32[256,256]{1,0:T(8,128)S(1)}) custom-call(f32[512,512]{1,0:T(8,128)S(1)} %invert_block.3.refs_0_, f32[512,256]{1,0:T(8,128)S(1)} %get-tuple-element.18.refs_1_, f32[512,512]{1,0:T(8,128)S(1)} %get-tuple-element.16.d_ref.refs_2_, ...), custom_call_target="tpu_custom_call" | custom-call | tf_op jit(solution)/shard_map/level_2/pallas_call | solution.py:412
  82.5 0.0 collective-permute-done.2.top_ref
  82.5 1.6 %finish.1 = (f32[512,256]{1,0:T(8,128)}, f32[512,256]{1,0:T(8,128)}, f32[64,512]{1,0:T(8,128)}) custom-call(f32[512,512]{1,0:T(8,128)S(1)} %get-tuple-element.21.carried_ref, f32[256,256]{1,0:T(8,128)S(1)} %collective-permute-done.2.top_ref, f32[256,256]{1,0:T(8,128)S(1)} %get-tuple-element.23.end_ref, f32[512,256]{1,0:T(8,128)S(1)} %get-tuple-element.24.diag_ref, ...), custom_call_target="tpu_custom_call" | custom-call | tf_op jit(solution)/shard_map/finish/pallas_call | solution.py:480
Async XLA Ops:
  0.6 33.8 %collective-permute-start = (f32[512,256]{1,0:T(8,128)}, f32[512,256]{1,0:T(8,128)S(1)}, u32[]{:S(2)}, u32[]{:S(2)}) collective-permute-start(f32[512,256]{1,0:T(8,128)} %bitcast.11), channel_id=1, source_target_pairs={{0,2},{2,4},{4,6},{6,8},{8,10},{10,12},{12,14},{14,16},{16,18},{18... | collective-permute-start | bytes 1572872 | tf_op jit(solution)/shard_map/ppermute | solution.py:492
  4.0 1.0 %copy-start = (f32[1,512,256]{2,1,0:T(8,128)S(1)}, f32[1,512,256]{2,1,0:T(8,128)}, u32[]{:S(2)}) copy-start(f32[1,512,256]{2,1,0:T(8,128)} %param.3) | copy-start | bytes 1572868
  7.7 5.9 %copy-start.1 = (f32[1,512,256]{2,1,0:T(8,128)S(1)}, f32[1,512,256]{2,1,0:T(8,128)}, u32[]{:S(2)}) copy-start(f32[1,512,256]{2,1,0:T(8,128)} %param.4) | copy-start | bytes 1572868
  7.7 5.9 %copy-start.2 = (f32[1,512,64]{1,2,0:T(8,128)S(1)}, f32[1,512,64]{1,2,0:T(8,128)}, u32[]{:S(2)}) copy-start(f32[1,512,64]{1,2,0:T(8,128)} %param.5) | copy-start | bytes 393220
  35.0 12.5 %collective-permute-start.1 = (f32[256,256]{1,0:T(8,128)S(1)}, f32[256,256]{1,0:T(8,128)S(1)}, u32[]{:S(2)}, u32[]{:S(2)}) collective-permute-start(f32[256,256]{1,0:T(8,128)S(1)} %get-tuple-element.20), channel_id=1, source_target_pairs={{0,6},{2,0},{4,2},{6,4},{8,14},{10,8},{12,10},{14,12},{16,22},{18,... | collective-permute-start | bytes 786440 | tf_op jit(solution)/shard_map/ppermute | solution.py:498
  36.9 45.6 %collective-permute-start.2 = (f32[256,256]{1,0:T(8,128)S(1)}, f32[256,256]{1,0:T(8,128)S(1)}, u32[]{:S(2)}, u32[]{:S(2)}) collective-permute-start(f32[256,256]{1,0:T(8,128)S(1)} %get-tuple-element.22), channel_id=1, source_target_pairs={{0,4},{2,6},{4,8},{6,10},{8,12},{10,14},{12,16},{14,18},{16,20},{1... | collective-permute-start | bytes 786440 | tf_op jit(solution)/shard_map/ppermute | solution.py:492

commit v6 on v4

--- a/solution.py
+++ b/solution.py
@@ -240,22 +240,15 @@
 
 def level_kernel(
     stride, last, p_ref, low_ref, diag_ref, rhs_ref, diag_out, rhs_out, carried_out,
-    low_full, p_out, p_in, p_full, t_own, t_out, t_in, t_full, t_rhs_in, rhs_in, *rest,
+    low_full, p_out, p_in, p_full, t_own, t_out, t_in, t_full, t_rhs_in, rhs_in, sems,
 ):
-    relay = stride > 1
-    if relay:
-        p_relay, t_relay, rhs_relay, t_rhs_relay, sems = rest
-    else:
-        (sems,) = rest
     length = lax.axis_size("tm")
-    row, core, up, down, sibling = neighbours(1)
+    row, core, up, down, sibling = neighbours(stride)
     size, width = low_ref.shape
     first = pl.multiple_of(core * width, width)
     mine = pl.ds(first, width)
     has_up = has_above = row + stride < length
     has_down = has_below = row >= stride
-    near_up, near_down = row + 1 < length, row >= 1
-    between = jnp.logical_and(near_up, near_down)
 
     barrier = pltpu.get_barrier_semaphore()
 
@@ -263,13 +256,13 @@
         pl.semaphore_signal(barrier, inc=1, device_id=device, device_id_type=MESH)
 
     signal(sibling)
-    pl.when(near_up)(lambda: signal(up))
-    pl.when(near_down)(lambda: signal(down))
+    pl.when(has_up)(lambda: signal(up))
+    pl.when(has_down)(lambda: signal(down))
     low_full[:, mine] = low_ref[...]
     pack_near(p_ref, 2 * core, core, p_out)
     pack_far(p_ref, 2 * core, core, p_out)
     pl.semaphore_wait(
-        barrier, 1 + near_up.astype(jnp.int32) + near_down.astype(jnp.int32)
+        barrier, 1 + has_up.astype(jnp.int32) + has_down.astype(jnp.int32)
     )
 
     used = iter(range(sems.shape[1]))
@@ -285,26 +278,18 @@
             device_id_type=MESH,
         )
 
-    def path(src, held, dst, device):
-        if not relay:
-            return [copy(src, dst, device)]
-        return [copy(src, held, device), copy(held, dst, device)]
-
-    def packed_paths(out, held, into, device):
+    def packed_copies(out, into, device):
         parts = [pl.ds(at, n) for at, n in CHUNKS]
-        return [
-            path(out.at[part], relay and held.at[part], into.at[core, part], device)
-            for part in parts
-        ]
+        return [copy(out.at[part], into.at[core, part], device) for part in parts]
 
     def packed_across(into):
         parts = [into.at[core, pl.ds(at, n)] for at, n in CHUNKS]
         return [copy(part, part, sibling) for part in parts]
 
-    p_paths = packed_paths(p_out, relay and p_relay, p_in, up)
-    t_paths = packed_paths(t_out, relay and t_relay, t_in, down)
-    p_paths.append(path(rhs_ref, relay and rhs_relay, rhs_in, up))
-    t_paths.append(path(t_own.at[width:], relay and t_rhs_relay, t_rhs_in, down))
+    p_copies = packed_copies(p_out, p_in, up)
+    t_copies = packed_copies(t_out, t_in, down)
+    rhs_copy = copy(rhs_ref, rhs_in, up)
+    t_rhs_copy = copy(t_own.at[width:], t_rhs_in, down)
     p_across, t_across = packed_across(p_in), packed_across(t_in)
     low_across = copy(low_ref, low_full.at[:, mine], sibling)
 
@@ -313,30 +298,22 @@
             getattr(one, call)()
 
     low_across.start()
-    pl.when(has_up)(lambda: each([way[0] for way in p_paths], "start"))
+    pl.when(has_up)(lambda: each(p_copies + [rhs_copy], "start"))
     own = halves(jnp.concatenate([low_ref[...].T, rhs_ref[...]], axis=0))
     own = halves(dot3(own, halves(p_ref[...])))
     t_own[:, mine] = dot3(own, halves(low_ref[...]))
     pack_near(t_own, 0, core, t_out)
-    pl.when(has_down)(t_paths[0][0].start)
+    pl.when(has_down)(t_copies[0].start)
     low_across.wait()
     others = pl.ds(pl.multiple_of((1 - core) * width, width), width)
     t_own[:, others] = dot3(own, halves(low_full[:, others]))
     pack_far(t_own, 0, core, t_out)
-    pl.when(has_down)(lambda: each([way[0] for way in t_paths[1:]], "start"))
+    pl.when(has_down)(lambda: each(t_copies[1:] + [t_rhs_copy], "start"))
     low = halves(low_full[...])
-    if relay:
-
-        @pl.when(between)
-        def _():
-            for way in p_paths[:2] + t_paths[:1] + p_paths[2:] + t_paths[1:]:
-                way[0].wait_recv()
-                way[1].start()
-
     @pl.when(has_below)
     def _():
-        for way, across in zip(p_paths, p_across):
-            way[-1].wait_recv()
+        for one, across in zip(p_copies, p_across):
+            one.wait_recv()
             across.start()
         each(p_across, "wait_recv")
 
@@ -346,13 +323,13 @@
     carried = halves(carried)
     from_diag = dot3(carried, low, NT)
     left = diag_ref[...] - jnp.where(has_below, from_diag, 0.0)
-    pl.when(has_below)(p_paths[-1][-1].wait_recv)
+    pl.when(has_below)(rhs_copy.wait_recv)
     from_rhs = dot3(halves(rhs_in[...]), carried, NT)
 
     @pl.when(has_above)
     def _():
-        for way, across in zip(t_paths, t_across):
-            way[-1].wait_recv()
+        for one, across in zip(t_copies, t_across):
+            one.wait_recv()
             across.start()
         each(t_across, "wait_recv")
 
@@ -362,16 +339,14 @@
         diag_out[...] = t_full[:, mine]
     else:
         diag_out[...] = left - jnp.where(has_above, t_full[...], 0.0)
-    pl.when(has_above)(t_paths[-1][-1].wait_recv)
+    pl.when(has_above)(t_rhs_copy.wait_recv)
     rhs_out[...] = (
         rhs_ref[...]
         - jnp.where(has_below, from_rhs, 0.0)
         - jnp.where(has_above, t_rhs_in[...], 0.0)
     )
-    pl.when(has_up)(lambda: each([way[0] for way in p_paths], "wait_send"))
-    pl.when(has_down)(lambda: each([way[0] for way in t_paths], "wait_send"))
-    if relay:
-        pl.when(between)(lambda: each([way[1] for way in p_paths + t_paths], "wait_send"))
+    pl.when(has_up)(lambda: each(p_copies + [rhs_copy], "wait_send"))
+    pl.when(has_down)(lambda: each(t_copies + [t_rhs_copy], "wait_send"))
     pl.when(has_below)(lambda: each(p_across, "wait_send"))
     pl.when(has_above)(lambda: each(t_across, "wait_send"))
 
@@ -384,8 +359,7 @@
     share = VMEM((PACKED, BLOCK), F32)
     shares = VMEM((2, PACKED, BLOCK), F32)
     vectors = VMEM((seqs, size), F32)
-    relays = [share, share, vectors, vectors]
-    copies = 4 * len(CHUNKS) + 3 + (2 * len(CHUNKS) + 2) * (stride > 1)
+    copies = 4 * len(CHUNKS) + 3
     return pl.pallas_call(
         functools.partial(level_kernel, stride, last),
         out_shape=(half if last else full, jax.ShapeDtypeStruct((seqs, size), F32), full),
@@ -402,7 +376,6 @@
             VMEM((size, size), F32),
             vectors,
             vectors,
-            *(relays if stride > 1 else ()),
             pltpu.SemaphoreType.DMA((2, copies)),
         ],
         compiler_params=pltpu.CompilerParams(

time: 79.1 us -> 74 us (0.936)
  the two profiles are of different devices: /device:TPU:256 before, /device:TPU:134 now
where the time goes in v6:
time: 74 us; the launch traced here: 73.7 us
  Pallas kernels  63.4 us (86%)
  starting transfers between devices  8.56 us (12%)
  local copies, waits for them, and re-layouts  1.05 us (1%)
  between operations  0.75 us (1%)
    pallas_call x2, Pallas kernels, level(): pl.pallas_call(functools.partial(level_kernel, stride, last), out_shape=(...  46.6 us
    pallas_call x2, Pallas kernels, invert(): pl.pallas_call(invert_kernel, out_shape=jax.ShapeDtypeStruct((size, size)...  11.9 us
    ppermute x2, starting transfers between devices, passed_up(): lax.ppermute(array, 'tm', [(i, i + stride) for i in range(length - stride)])  8.56 us
    pallas_call x1, Pallas kernels, join(): pl.pallas_call(join_kernel, out_shape=jax.ShapeDtypeStruct((size, 2 * wid...  2.64 us
    pallas_call x1, Pallas kernels, finish(): pl.pallas_call(functools.partial(finish_kernel, stride), out_shape=(half,...  1.56 us
  transfers between devices with their start and end apart: 2, of which 0 were waited for; matrix products, arithmetic and copies ran while one was open for 0% of the time, Pallas kernels for 83%

profile of v6, /device:TPU:134, one launch (start us, length us, event | category | flops | bytes accessed | tf_op | source)
XLA Modules:
  0.0 73.7 jit_solution(10731333680366364795)
XLA Ops:
  0.6 3.4 %collective-permute-start = (f32[512,256]{1,0:T(8,128)}, f32[512,256]{1,0:T(8,128)S(1)}, u32[]{:S(2)}, u32[]{:S(2)}) collective-permute-start(f32[512,256]{1,0:T(8,128)} %bitcast.11), channel_id=1, source_target_pairs={{0,2},{2,4},{4,6},{6,8},{8,10},{10,12},{12,14},{14,16},{16,18},{18... | collective-permute-start | bytes 1572872 | tf_op jit(solution)/shard_map/ppermute | solution.py:424
  4.0 0.0 copy-start
  4.0 1.0 %copy-done = f32[1,512,256]{2,1,0:T(8,128)S(1)} copy-done((f32[1,512,256]{2,1,0:T(8,128)S(1)}, f32[1,512,256]{2,1,0:T(8,128)}, u32[]{:S(2)}) %copy-start) | copy-done | bytes 524312
  5.1 2.6 %join_halves.1.d_ref.diag_ref = f32[512,512]{1,0:T(8,128)S(1)} custom-call(f32[512,256]{1,0:T(8,128)S(1)} %bitcast.10), custom_call_target="tpu_custom_call" | custom-call | tf_op jit(solution)/shard_map/join_halves/pallas_call | solution.py:80
  7.7 0.0 copy-start.1
  7.7 0.0 copy-start.2
  7.8 5.9 %invert_block.2.p_ref = f32[512,512]{1,0:T(8,128)S(1)} custom-call(f32[512,512]{1,0:T(8,128)S(1)} %join_halves.1.d_ref.diag_ref), custom_call_target="tpu_custom_call" | custom-call | flops 3221225472 | bytes 2097152 | tf_op jit(solution)/shard_map/invert_block/pallas_call | solution.py:175
  13.6 0.0 copy-done.1
  13.6 0.0 copy-done.2
  13.7 15.6 %level_1.1 = (f32[512,512]{1,0:T(8,128)S(1)}, f32[64,512]{1,0:T(8,128)S(1)}, f32[512,512]{1,0:T(8,128)S(1)}) custom-call(f32[512,512]{1,0:T(8,128)S(1)} %invert_block.2.p_ref, f32[512,256]{1,0:T(8,128)S(1)} %bitcast.12, f32[512,512]{1,0:T(8,128)S(1)} %join_halves.1.d_ref.diag_ref, f32[64,512]{1,0:T(8,128)S(1)} %bitcast.13), custom_call_target="tpu_custom_call" | custom-call | tf_op jit(solution)/shard_map/level_1/pallas_call | solution.py:363
  29.3 0.0 collective-permute-done.low_prev_ref
  29.3 0.6 couple.1.low_ref
  29.9 5.2 %collective-permute-start.1 = (f32[512,256]{1,0:T(8,128)S(1)}, f32[512,256]{1,0:T(8,128)S(1)}, u32[]{:S(2)}, u32[]{:S(2)}) collective-permute-start(f32[512,256]{1,0:T(8,128)S(1)} %couple.1.low_ref), channel_id=1, source_target_pairs={{0,4},{2,6},{4,8},{6,10},{8,12},{10,14},{12,16},{14,18},{16,20},{1... | collective-permute-start | bytes 1572872 | tf_op jit(solution)/shard_map/ppermute | solution.py:424
  35.0 6.1 %invert_block.3.p_ref = f32[512,512]{1,0:T(8,128)S(1)} custom-call(f32[512,512]{1,0:T(8,128)S(1)} %get-tuple-element.12.d_ref.diag_ref), custom_call_target="tpu_custom_call" | custom-call | flops 3221225472 | bytes 2097152 | tf_op jit(solution)/shard_map/invert_block/pallas_call | solution.py:175
  41.1 31.0 %level_2.1 = (f32[512,256]{1,0:T(8,128)S(1)}, f32[64,512]{1,0:T(8,128)S(1)}, f32[512,512]{1,0:T(8,128)S(1)}) custom-call(f32[512,512]{1,0:T(8,128)S(1)} %invert_block.3.p_ref, f32[512,256]{1,0:T(8,128)S(1)} %couple.1.low_ref, f32[512,512]{1,0:T(8,128)S(1)} %get-tuple-element.12.d_ref.diag_ref, f32[64,512]{1,0:T(8,128)S(1)} %get-tuple-element.14.rhs_ref), custom_call_target="tpu_custom_call" | custom-call | tf_op jit(solution)/shard_map/level_2/pallas_call | solution.py:363
  72.1 0.0 collective-permute-done.1.low_prev_ref
  72.2 1.6 %finish.1 = (f32[512,256]{1,0:T(8,128)}, f32[512,256]{1,0:T(8,128)}, f32[64,512]{1,0:T(8,128)}) custom-call(f32[512,512]{1,0:T(8,128)S(1)} %get-tuple-element.15.carried_ref, f32[512,256]{1,0:T(8,128)S(1)} %collective-permute-done.1.low_prev_ref, f32[512,256]{1,0:T(8,128)S(1)} %get-tuple-element.16.diag_ref, f32[64,512]{1,0:T(8,128)S(1)} %get-tuple-element.17.rhs_ref), custom_call_target="tpu_custom_call" | custom-call | tf_op jit(solution)/shard_map/finish/pallas_call | solution.py:412
Async XLA Ops:
  0.6 28.6 %collective-permute-start = (f32[512,256]{1,0:T(8,128)}, f32[512,256]{1,0:T(8,128)S(1)}, u32[]{:S(2)}, u32[]{:S(2)}) collective-permute-start(f32[512,256]{1,0:T(8,128)} %bitcast.11), channel_id=1, source_target_pairs={{0,2},{2,4},{4,6},{6,8},{8,10},{10,12},{12,14},{14,16},{16,18},{18... | collective-permute-start | bytes 1572872 | tf_op jit(solution)/shard_map/ppermute | solution.py:424
  4.0 1.0 %copy-start = (f32[1,512,256]{2,1,0:T(8,128)S(1)}, f32[1,512,256]{2,1,0:T(8,128)}, u32[]{:S(2)}) copy-start(f32[1,512,256]{2,1,0:T(8,128)} %param.3) | copy-start | bytes 1572868
  7.7 5.9 %copy-start.1 = (f32[1,512,256]{2,1,0:T(8,128)S(1)}, f32[1,512,256]{2,1,0:T(8,128)}, u32[]{:S(2)}) copy-start(f32[1,512,256]{2,1,0:T(8,128)} %param.4) | copy-start | bytes 1572868
  7.7 5.9 %copy-start.2 = (f32[1,512,64]{1,2,0:T(8,128)S(1)}, f32[1,512,64]{1,2,0:T(8,128)}, u32[]{:S(2)}) copy-start(f32[1,512,64]{1,2,0:T(8,128)} %param.5) | copy-start | bytes 393220
  29.9 42.3 %collective-permute-start.1 = (f32[512,256]{1,0:T(8,128)S(1)}, f32[512,256]{1,0:T(8,128)S(1)}, u32[]{:S(2)}, u32[]{:S(2)}) collective-permute-start(f32[512,256]{1,0:T(8,128)S(1)} %couple.1.low_ref), channel_id=1, source_target_pairs={{0,4},{2,6},{4,8},{6,10},{8,12},{10,14},{12,16},{14,18},{16,20},{1... | collective-permute-start | bytes 1572872 | tf_op jit(solution)/shard_map/ppermute | solution.py:424

commit v7 on v6

--- a/solution.py
+++ b/solution.py
@@ -238,10 +238,11 @@
         put(2 * core + 1, 2 * core + 1, second)
 
 
-def level_kernel(
-    stride, last, p_ref, low_ref, diag_ref, rhs_ref, diag_out, rhs_out, carried_out,
-    low_full, p_out, p_in, p_full, t_own, t_out, t_in, t_full, t_rhs_in, rhs_in, sems,
-):
+def level_kernel(stride, last, *refs):
+    p_ref, low_ref, diag_ref, rhs_ref, diag_out, rhs_out, carried_out, *refs = refs
+    if last:
+        low_prev_out, *refs = refs
+    low_full, p_out, p_in, p_full, t_own, t_out, t_in, t_full, t_rhs_in, rhs_in, sems = refs
     length = lax.axis_size("tm")
     row, core, up, down, sibling = neighbours(stride)
     size, width = low_ref.shape
@@ -292,6 +293,8 @@
     t_rhs_copy = copy(t_own.at[width:], t_rhs_in, down)
     p_across, t_across = packed_across(p_in), packed_across(t_in)
     low_across = copy(low_ref, low_full.at[:, mine], sibling)
+    if last:
+        low_copy = copy(low_ref, low_prev_out, up)
 
     def each(copies, call):
         for one in copies:
@@ -309,6 +312,8 @@
     t_own[:, others] = dot3(own, halves(low_full[:, others]))
     pack_far(t_own, 0, core, t_out)
     pl.when(has_down)(lambda: each(t_copies[1:] + [t_rhs_copy], "start"))
+    if last:
+        pl.when(has_up)(low_copy.start)
     low = halves(low_full[...])
     @pl.when(has_below)
     def _():
@@ -349,6 +354,9 @@
     pl.when(has_down)(lambda: each(t_copies + [t_rhs_copy], "wait_send"))
     pl.when(has_below)(lambda: each(p_across, "wait_send"))
     pl.when(has_above)(lambda: each(t_across, "wait_send"))
+    if last:
+        pl.when(has_up)(low_copy.wait_send)
+        pl.when(has_below)(low_copy.wait_recv)
 
 
 def level(stride, last, p, low_cols, diag, rhs):
@@ -359,12 +367,16 @@
     share = VMEM((PACKED, BLOCK), F32)
     shares = VMEM((2, PACKED, BLOCK), F32)
     vectors = VMEM((seqs, size), F32)
-    copies = 4 * len(CHUNKS) + 3
+    copies = 4 * len(CHUNKS) + 3 + last
+    out_shape = [half if last else full, jax.ShapeDtypeStruct((seqs, size), F32), full]
+    if last:
+        out_shape.append(half)
+    in_vmem = pl.BlockSpec(memory_space=VMEM)
     return pl.pallas_call(
         functools.partial(level_kernel, stride, last),
-        out_shape=(half if last else full, jax.ShapeDtypeStruct((seqs, size), F32), full),
-        in_specs=[pl.BlockSpec(memory_space=VMEM)] * 4,
-        out_specs=[pl.BlockSpec(memory_space=VMEM)] * 3,
+        out_shape=out_shape,
+        in_specs=[in_vmem] * 4,
+        out_specs=[in_vmem] * len(out_shape),
         scratch_shapes=[
             VMEM((size, size), F32),
             share,
@@ -430,8 +442,7 @@
     diag = join(diagonal[0])
     diag, rhs_rows, carried = level(1, False, invert(diag), low_cols, diag, rhs_rows)
     low_cols = couple(1, carried, low_prev)
-    low_prev = passed_up(low_cols, 2)
-    diag, rhs_rows, carried = level(2, True, invert(diag), low_cols, diag, rhs_rows)
+    diag, rhs_rows, carried, low_prev = level(2, True, invert(diag), low_cols, diag, rhs_rows)
     diag, low_cols, rhs_rows = finish(2, carried, low_prev, diag, rhs_rows)
     return diag[None], low_cols[None], rhs_rows.T[None]
 

time: 74 us -> 77.2 us (1.043)
  the two profiles are of different devices: /device:TPU:134 before, /device:TPU:152 now
where the time goes in v7:
time: 77.2 us; the launch traced here: 77 us
  Pallas kernels  71.8 us (93%)
  starting transfers between devices  3.4 us (4%)
  local copies, waits for them, and re-layouts  1.05 us (1%)
    pallas_call x2, Pallas kernels, level(): pl.pallas_call(functools.partial(level_kernel, stride, last), out_shape=o...  55 us
    pallas_call x2, Pallas kernels, invert(): pl.pallas_call(invert_kernel, out_shape=jax.ShapeDtypeStruct((size, size)...  12 us
    ppermute x1, starting transfers between devices, passed_up(): lax.ppermute(array, 'tm', [(i, i + stride) for i in range(length - stride)])  3.4 us
    pallas_call x1, Pallas kernels, join(): pl.pallas_call(join_kernel, out_shape=jax.ShapeDtypeStruct((size, 2 * wid...  2.64 us
    pallas_call x1, Pallas kernels, finish(): pl.pallas_call(functools.partial(finish_kernel, stride), out_shape=(half,...  1.55 us
  transfers between devices with their start and end apart: 1, of which 0 were waited for; matrix products, arithmetic and copies ran while one was open for 0% of the time, Pallas kernels for 42%

profile of v7, /device:TPU:152, one launch (start us, length us, event | category | flops | bytes accessed | tf_op | source)
XLA Modules:
  0.0 77.0 jit_solution(707085823687304442)
XLA Ops:
  0.6 3.4 %collective-permute-start = (f32[512,256]{1,0:T(8,128)}, f32[512,256]{1,0:T(8,128)S(1)}, u32[]{:S(2)}, u32[]{:S(2)}) collective-permute-start(f32[512,256]{1,0:T(8,128)} %bitcast.11), channel_id=1, source_target_pairs={{0,2},{2,4},{4,6},{6,8},{8,10},{10,12},{12,14},{14,16},{16,18},{18... | collective-permute-start | bytes 1572872 | tf_op jit(solution)/shard_map/ppermute | solution.py:436
  4.0 0.0 copy-start
  4.0 1.0 %copy-done = f32[1,512,256]{2,1,0:T(8,128)S(1)} copy-done((f32[1,512,256]{2,1,0:T(8,128)S(1)}, f32[1,512,256]{2,1,0:T(8,128)}, u32[]{:S(2)}) %copy-start) | copy-done | bytes 524312
  5.1 2.6 %join_halves.1.d_ref.refs_2_ = f32[512,512]{1,0:T(8,128)S(1)} custom-call(f32[512,256]{1,0:T(8,128)S(1)} %bitcast.10), custom_call_target="tpu_custom_call" | custom-call | tf_op jit(solution)/shard_map/join_halves/pallas_call | solution.py:80
  7.7 0.0 copy-start.1
  7.7 0.0 copy-start.2
  7.8 5.9 %invert_block.2.refs_0_ = f32[512,512]{1,0:T(8,128)S(1)} custom-call(f32[512,512]{1,0:T(8,128)S(1)} %join_halves.1.d_ref.refs_2_), custom_call_target="tpu_custom_call" | custom-call | flops 3221225472 | bytes 2097152 | tf_op jit(solution)/shard_map/invert_block/pallas_call | solution.py:175
  13.7 0.0 copy-done.1
  13.7 0.0 copy-done.2
  13.7 17.4 %level_1.1 = (f32[512,512]{1,0:T(8,128)S(1)}, f32[64,512]{1,0:T(8,128)S(1)}, f32[512,512]{1,0:T(8,128)S(1)}) custom-call(f32[512,512]{1,0:T(8,128)S(1)} %invert_block.2.refs_0_, f32[512,256]{1,0:T(8,128)S(1)} %bitcast.12, f32[512,512]{1,0:T(8,128)S(1)} %join_halves.1.d_ref.refs_2_, f32[64,512]{1,0:T(8,128)S(1)} %bitcast.13), custom_call_target="tpu_custom_call" | custom-call | tf_op jit(solution)/shard_map/level_1/pallas_call | solution.py:375
  31.1 6.1 %invert_block.3.refs_0_ = f32[512,512]{1,0:T(8,128)S(1)} custom-call(f32[512,512]{1,0:T(8,128)S(1)} %get-tuple-element.13.d_ref.refs_2_), custom_call_target="tpu_custom_call" | custom-call | flops 3221225472 | bytes 2097152 | tf_op jit(solution)/shard_map/invert_block/pallas_call | solution.py:175
  37.1 0.0 collective-permute-done.low_prev_ref
  37.2 0.6 couple.1.refs_1_
  37.8 37.6 %level_2.1 = (f32[512,256]{1,0:T(8,128)S(1)}, f32[64,512]{1,0:T(8,128)S(1)}, f32[512,512]{1,0:T(8,128)S(1)}, f32[512,256]{1,0:T(8,128)S(1)}) custom-call(f32[512,512]{1,0:T(8,128)S(1)} %invert_block.3.refs_0_, f32[512,256]{1,0:T(8,128)S(1)} %couple.1.refs_1_, f32[512,512]{1,0:T(8,128)S(1)} %get-tuple-element.13.d_ref.refs_2_, ...), custom_call_target="tpu_custom_call" | custom-call | tf_op jit(solution)/shard_map/level_2/pallas_call | solution.py:375
  75.4 1.5 %finish.1 = (f32[512,256]{1,0:T(8,128)}, f32[512,256]{1,0:T(8,128)}, f32[64,512]{1,0:T(8,128)}) custom-call(f32[512,512]{1,0:T(8,128)S(1)} %get-tuple-element.16.carried_ref, f32[512,256]{1,0:T(8,128)S(1)} %get-tuple-element.17.low_prev_ref, f32[512,256]{1,0:T(8,128)S(1)} %get-tuple-element.18.diag_ref, f32[64,512]{1,0:T(8,128)S(1)} %get-tuple-element.19.rhs_ref), custom_call_target="tpu_custom_call" | custom-call | tf_op jit(solution)/shard_map/finish/pallas_call | solution.py:424
Async XLA Ops:
  0.6 36.5 %collective-permute-start = (f32[512,256]{1,0:T(8,128)}, f32[512,256]{1,0:T(8,128)S(1)}, u32[]{:S(2)}, u32[]{:S(2)}) collective-permute-start(f32[512,256]{1,0:T(8,128)} %bitcast.11), channel_id=1, source_target_pairs={{0,2},{2,4},{4,6},{6,8},{8,10},{10,12},{12,14},{14,16},{16,18},{18... | collective-permute-start | bytes 1572872 | tf_op jit(solution)/shard_map/ppermute | solution.py:436
  4.0 1.0 %copy-start = (f32[1,512,256]{2,1,0:T(8,128)S(1)}, f32[1,512,256]{2,1,0:T(8,128)}, u32[]{:S(2)}) copy-start(f32[1,512,256]{2,1,0:T(8,128)} %param.3) | copy-start | bytes 1572868
  7.7 5.9 %copy-start.1 = (f32[1,512,256]{2,1,0:T(8,128)S(1)}, f32[1,512,256]{2,1,0:T(8,128)}, u32[]{:S(2)}) copy-start(f32[1,512,256]{2,1,0:T(8,128)} %param.4) | copy-start | bytes 1572868
  7.7 5.9 %copy-start.2 = (f32[1,512,64]{1,2,0:T(8,128)S(1)}, f32[1,512,64]{1,2,0:T(8,128)}, u32[]{:S(2)}) copy-start(f32[1,512,64]{1,2,0:T(8,128)} %param.5) | copy-start | bytes 393220

commit v8 on v7

--- a/solution.py
+++ b/solution.py
@@ -32,6 +32,13 @@
 
 def dot3(a, b, dims=NN):
     return dot1(a[0], b[0], dims) + (dot1(a[0], b[1], dims) + dot1(a[1], b[0], dims))
+
+
+RING = 4
+
+
+def row_at(row, turn):
+    return row - row % RING + (row + turn) % RING
 
 
 def neighbours(stride):
@@ -241,7 +248,7 @@
 def level_kernel(stride, last, *refs):
     p_ref, low_ref, diag_ref, rhs_ref, diag_out, rhs_out, carried_out, *refs = refs
     if last:
-        low_prev_out, *refs = refs
+        top_out, end_out, held, *refs = refs
     low_full, p_out, p_in, p_full, t_own, t_out, t_in, t_full, t_rhs_in, rhs_in, sems = refs
     length = lax.axis_size("tm")
     row, core, up, down, sibling = neighbours(stride)
@@ -259,12 +266,18 @@
     signal(sibling)
     pl.when(has_up)(lambda: signal(up))
     pl.when(has_down)(lambda: signal(down))
+    waits = 1 + has_up.astype(jnp.int32) + has_down.astype(jnp.int32)
+    if last:
+        east, west = row_at(row, 1), row_at(row, RING - 1)
+        onward = east + stride
+        has_onward = onward < length
+        pl.when(has_onward)(lambda: signal((east, core)))
+        pl.when(has_below)(lambda: signal((row_at(row - stride, RING - 1), core)))
+        waits += has_up.astype(jnp.int32) + has_onward.astype(jnp.int32)
     low_full[:, mine] = low_ref[...]
     pack_near(p_ref, 2 * core, core, p_out)
     pack_far(p_ref, 2 * core, core, p_out)
-    pl.semaphore_wait(
-        barrier, 1 + has_up.astype(jnp.int32) + has_down.astype(jnp.int32)
-    )
+    pl.semaphore_wait(barrier, waits)
 
     used = iter(range(sems.shape[1]))
 
@@ -294,13 +307,18 @@
     p_across, t_across = packed_across(p_in), packed_across(t_in)
     low_across = copy(low_ref, low_full.at[:, mine], sibling)
     if last:
-        low_copy = copy(low_ref, low_prev_out, up)
+        cut = size // 2
+        top_copy = copy(low_ref.at[:cut], top_out, up)
+        west_copy = copy(low_ref.at[pl.ds(cut, cut)], held, (west, core))
+        end_copy = copy(held, end_out, (onward, core))
 
     def each(copies, call):
         for one in copies:
             getattr(one, call)()
 
     low_across.start()
+    if last:
+        pl.when(has_up)(west_copy.start)
     pl.when(has_up)(lambda: each(p_copies + [rhs_copy], "start"))
     own = halves(jnp.concatenate([low_ref[...].T, rhs_ref[...]], axis=0))
     own = halves(dot3(own, halves(p_ref[...])))
@@ -313,7 +331,13 @@
     pack_far(t_own, 0, core, t_out)
     pl.when(has_down)(lambda: each(t_copies[1:] + [t_rhs_copy], "start"))
     if last:
-        pl.when(has_up)(low_copy.start)
+        pl.when(has_up)(top_copy.start)
+
+        @pl.when(has_onward)
+        def _():
+            west_copy.wait_recv()
+            end_copy.start()
+
     low = halves(low_full[...])
     @pl.when(has_below)
     def _():
@@ -355,8 +379,9 @@
     pl.when(has_below)(lambda: each(p_across, "wait_send"))
     pl.when(has_above)(lambda: each(t_across, "wait_send"))
     if last:
-        pl.when(has_up)(low_copy.wait_send)
-        pl.when(has_below)(low_copy.wait_recv)
+        pl.when(has_up)(lambda: each([top_copy, west_copy], "wait_send"))
+        pl.when(has_onward)(end_copy.wait_send)
+        pl.when(has_below)(lambda: each([top_copy, end_copy], "wait_recv"))
 
 
 def level(stride, last, p, low_cols, diag, rhs):
@@ -367,10 +392,13 @@
     share = VMEM((PACKED, BLOCK), F32)
     shares = VMEM((2, PACKED, BLOCK), F32)
     vectors = VMEM((seqs, size), F32)
-    copies = 4 * len(CHUNKS) + 3 + last
+    copies = 4 * len(CHUNKS) + 3 + 3 * last
     out_shape = [half if last else full, jax.ShapeDtypeStruct((seqs, size), F32), full]
-    if last:
-        out_shape.append(half)
+    held = ()
+    if last:
+        part = (size // 2, width)
+        out_shape += [jax.ShapeDtypeStruct(part, F32)] * 2
+        held = (VMEM(part, F32),)
     in_vmem = pl.BlockSpec(memory_space=VMEM)
     return pl.pallas_call(
         functools.partial(level_kernel, stride, last),
@@ -378,6 +406,7 @@
         in_specs=[in_vmem] * 4,
         out_specs=[in_vmem] * len(out_shape),
         scratch_shapes=[
+            *held,
             VMEM((size, size), F32),
             share,
             shares,
@@ -397,9 +426,18 @@
     )(p, low_cols, diag, rhs)
 
 
+def coupling(stride, carried_ref, *low_prev):
+    carried = halves(carried_ref[...])
+    total, at = 0.0, 0
+    for part in low_prev:
+        rows = part.shape[0]
+        total += dot3([half[:, at : at + rows] for half in carried], halves(part[...]))
+        at += rows
+    return jnp.where(lax.axis_index("tm") >= 2 * stride, -total, 0.0)
+
+
 def couple_kernel(stride, carried_ref, low_prev_ref, low_out):
-    product = dot3(halves(carried_ref[...]), halves(low_prev_ref[...]))
-    low_out[...] = jnp.where(lax.axis_index("tm") >= 2 * stride, -product, 0.0)
+    low_out[...] = coupling(stride, carried_ref, low_prev_ref)
 
 
 def couple(stride, carried, low_prev):
@@ -413,22 +451,24 @@
     )(carried, low_prev)
 
 
-def finish_kernel(stride, carried_ref, low_prev_ref, diag_ref, rhs_ref, diag_out, low_out, rhs_out):
-    couple_kernel(stride, carried_ref, low_prev_ref, low_out)
+def finish_kernel(
+    stride, carried_ref, top_ref, end_ref, diag_ref, rhs_ref, diag_out, low_out, rhs_out
+):
+    low_out[...] = coupling(stride, carried_ref, top_ref, end_ref)
     diag_out[...] = diag_ref[...]
     rhs_out[...] = rhs_ref[...]
 
 
-def finish(stride, carried, low_prev, diag, rhs):
+def finish(stride, carried, top, end, diag, rhs):
     half = jax.ShapeDtypeStruct(diag.shape, F32)
     return pl.pallas_call(
         functools.partial(finish_kernel, stride),
         out_shape=(half, half, jax.ShapeDtypeStruct(rhs.shape, F32)),
-        in_specs=[pl.BlockSpec(memory_space=VMEM)] * 4,
+        in_specs=[pl.BlockSpec(memory_space=VMEM)] * 5,
         out_specs=[pl.BlockSpec(memory_space=VMEM)] * 3,
         compiler_params=pltpu.CompilerParams(vmem_limit_bytes=VMEM_LIMIT),
         name="finish",
-    )(carried, low_prev, diag, rhs)
+    )(carried, top, end, diag, rhs)
 
 
 def passed_up(array, stride):
@@ -442,8 +482,8 @@
     diag = join(diagonal[0])
     diag, rhs_rows, carried = level(1, False, invert(diag), low_cols, diag, rhs_rows)
     low_cols = couple(1, carried, low_prev)
-    diag, rhs_rows, carried, low_prev = level(2, True, invert(diag), low_cols, diag, rhs_rows)
-    diag, low_cols, rhs_rows = finish(2, carried, low_prev, diag, rhs_rows)
+    diag, rhs_rows, carried, *low_prev = level(2, True, invert(diag), low_cols, diag, rhs_rows)
+    diag, low_cols, rhs_rows = finish(2, carried, *low_prev, diag, rhs_rows)
     return diag[None], low_cols[None], rhs_rows.T[None]
 
 

time: 77.2 us -> 89.8 us (1.16)
  the two profiles are of different devices: /device:TPU:152 before, /device:TPU:64 now
where the time goes in v8:
time: 89.8 us; the launch traced here: 89.6 us
  Pallas kernels  84.4 us (94%)
  starting transfers between devices  3.4 us (4%)
  local copies, waits for them, and re-layouts  1.05 us (1%)
    pallas_call x2, Pallas kernels, level(): pl.pallas_call(functools.partial(level_kernel, stride, last), out_shape=o...  67.7 us
    pallas_call x2, Pallas kernels, invert(): pl.pallas_call(invert_kernel, out_shape=jax.ShapeDtypeStruct((size, size)...  12 us
    ppermute x1, starting transfers between devices, passed_up(): lax.ppermute(array, 'tm', [(i, i + stride) for i in range(length - stride)])  3.4 us
    pallas_call x1, Pallas kernels, join(): pl.pallas_call(join_kernel, out_shape=jax.ShapeDtypeStruct((size, 2 * wid...  2.64 us
  transfers between devices with their start and end apart: 1, of which 0 were waited for; matrix products, arithmetic and copies ran while one was open for 0% of the time, Pallas kernels for 38%

profile of v8, /device:TPU:64, one launch (start us, length us, event | category | flops | bytes accessed | tf_op | source)
XLA Modules:
  0.0 89.6 jit_solution(14902623811998104326)
XLA Ops:
  0.6 3.4 %collective-permute-start = (f32[512,256]{1,0:T(8,128)}, f32[512,256]{1,0:T(8,128)S(1)}, u32[]{:S(2)}, u32[]{:S(2)}) collective-permute-start(f32[512,256]{1,0:T(8,128)} %bitcast.11), channel_id=1, source_target_pairs={{0,2},{2,4},{4,6},{6,8},{8,10},{10,12},{12,14},{14,16},{16,18},{18... | collective-permute-start | bytes 1572872 | tf_op jit(solution)/shard_map/ppermute | solution.py:476
  4.0 0.0 copy-start
  4.0 1.0 %copy-done = f32[1,512,256]{2,1,0:T(8,128)S(1)} copy-done((f32[1,512,256]{2,1,0:T(8,128)S(1)}, f32[1,512,256]{2,1,0:T(8,128)}, u32[]{:S(2)}) %copy-start) | copy-done | bytes 524312
  5.1 2.6 %join_halves.1.d_ref.refs_2_ = f32[512,512]{1,0:T(8,128)S(1)} custom-call(f32[512,256]{1,0:T(8,128)S(1)} %bitcast.10), custom_call_target="tpu_custom_call" | custom-call | tf_op jit(solution)/shard_map/join_halves/pallas_call | solution.py:87
  7.7 0.0 copy-start.1
  7.7 0.0 copy-start.2
  7.8 5.9 %invert_block.2.refs_0_ = f32[512,512]{1,0:T(8,128)S(1)} custom-call(f32[512,512]{1,0:T(8,128)S(1)} %join_halves.1.d_ref.refs_2_), custom_call_target="tpu_custom_call" | custom-call | flops 3221225472 | bytes 2097152 | tf_op jit(solution)/shard_map/invert_block/pallas_call | solution.py:182
  13.7 0.0 copy-done.1
  13.7 0.0 copy-done.2
  13.7 19.5 %level_1.1 = (f32[512,512]{1,0:T(8,128)S(1)}, f32[64,512]{1,0:T(8,128)S(1)}, f32[512,512]{1,0:T(8,128)S(1)}) custom-call(f32[512,512]{1,0:T(8,128)S(1)} %invert_block.2.refs_0_, f32[512,256]{1,0:T(8,128)S(1)} %bitcast.12, f32[512,512]{1,0:T(8,128)S(1)} %join_halves.1.d_ref.refs_2_, f32[64,512]{1,0:T(8,128)S(1)} %bitcast.13), custom_call_target="tpu_custom_call" | custom-call | tf_op jit(solution)/shard_map/level_1/pallas_call | solution.py:403
  33.2 6.1 %invert_block.3.refs_0_ = f32[512,512]{1,0:T(8,128)S(1)} custom-call(f32[512,512]{1,0:T(8,128)S(1)} %get-tuple-element.14.d_ref.refs_2_), custom_call_target="tpu_custom_call" | custom-call | flops 3221225472 | bytes 2097152 | tf_op jit(solution)/shard_map/invert_block/pallas_call | solution.py:182
  39.3 0.0 collective-permute-done.low_prev_ref
  39.3 0.6 couple.1.refs_1_
  39.9 48.2 %level_2.1 = (f32[512,256]{1,0:T(8,128)S(1)}, f32[64,512]{1,0:T(8,128)S(1)}, f32[512,512]{1,0:T(8,128)S(1)}, f32[256,256]{1,0:T(8,128)S(1)}, f32[256,256]{1,0:T(8,128)S(1)}) custom-call(f32[512,512]{1,0:T(8,128)S(1)} %invert_block.3.refs_0_, f32[512,256]{1,0:T(8,128)S(1)} %couple.1.refs_1_, f32[512,512]{1,0:T(8,128)S(1)} %get-tuple-element.14.d_ref.refs_2_, ...), custom_call_target="tpu_custom_call" | custom-call | tf_op jit(solution)/shard_map/level_2/pallas_call | solution.py:403
  88.0 1.6 %finish.1 = (f32[512,256]{1,0:T(8,128)}, f32[512,256]{1,0:T(8,128)}, f32[64,512]{1,0:T(8,128)}) custom-call(f32[512,512]{1,0:T(8,128)S(1)} %get-tuple-element.17.carried_ref, f32[256,256]{1,0:T(8,128)S(1)} %get-tuple-element.18.top_ref, f32[256,256]{1,0:T(8,128)S(1)} %get-tuple-element.19.end_ref, f32[512,256]{1,0:T(8,128)S(1)} %get-tuple-element.20.diag_ref, ...), custom_call_target="tpu_custom_call" | custom-call | tf_op jit(solution)/shard_map/finish/pallas_call | solution.py:464
Async XLA Ops:
  0.6 38.6 %collective-permute-start = (f32[512,256]{1,0:T(8,128)}, f32[512,256]{1,0:T(8,128)S(1)}, u32[]{:S(2)}, u32[]{:S(2)}) collective-permute-start(f32[512,256]{1,0:T(8,128)} %bitcast.11), channel_id=1, source_target_pairs={{0,2},{2,4},{4,6},{6,8},{8,10},{10,12},{12,14},{14,16},{16,18},{18... | collective-permute-start | bytes 1572872 | tf_op jit(solution)/shard_map/ppermute | solution.py:476
  4.0 1.0 %copy-start = (f32[1,512,256]{2,1,0:T(8,128)S(1)}, f32[1,512,256]{2,1,0:T(8,128)}, u32[]{:S(2)}) copy-start(f32[1,512,256]{2,1,0:T(8,128)} %param.3) | copy-start | bytes 1572868
  7.7 5.9 %copy-start.1 = (f32[1,512,256]{2,1,0:T(8,128)S(1)}, f32[1,512,256]{2,1,0:T(8,128)}, u32[]{:S(2)}) copy-start(f32[1,512,256]{2,1,0:T(8,128)} %param.4) | copy-start | bytes 1572868
  7.7 5.9 %copy-start.2 = (f32[1,512,64]{1,2,0:T(8,128)S(1)}, f32[1,512,64]{1,2,0:T(8,128)}, u32[]{:S(2)}) copy-start(f32[1,512,64]{1,2,0:T(8,128)} %param.5) | copy-start | bytes 393220
